TPU v7x, 32 devices: a whole 2x2x4 slice. The times are simulated.
32 devices in a mesh: cfg: 2 (over x), seq: 16 (over z, y, core).
Axes of the slice: x: 2, y: 2, z: 4, core: 2. Of those that a mesh axis runs over, the one named last changes fastest.
Arguments:
- img_queries: bfloat16 [2, 192, 1216], P('cfg', 'seq')
- img_keys: bfloat16 [2, 192, 1216], P('cfg', 'seq')
- img_values: bfloat16 [2, 192, 1216], P('cfg', 'seq'), may hold values from -6 to 6
- text_keys: bfloat16 [2, 16, 1216], P('cfg', 'seq'), may hold values from -6 to 6
- text_values: bfloat16 [2, 16, 1216], P('cfg', 'seq'), may hold values from -18 to 18
- query_gain: float32 [64], replicated, may hold values from 0.5 to 8, as said below
- key_gain: float32 [64], replicated, may hold values from 0.5 to 8, as said below
- text_gain: float32 [64], replicated, may hold values from 0.5 to 8, as said below
- text_lengths: int32 [2], P('cfg'), may hold values from 1 to 16, as said below
- text_blocks: int32 [2, 16], P('cfg', 'seq'), may hold values from 0 to 1
- latent: float32 [192, 64], P('seq', 'cfg'), may hold values from -6 to 6
- base_velocity: bfloat16 [2, 192, 64], P('cfg', 'seq'), may hold values from -6 to 6
- out_weight: bfloat16 [1216, 64], replicated, may hold values from -1.25 to 1.25
- timestep: int32 [1], replicated, may hold values from 0 to 27
Outputs:
- next_latent: float32 [192, 64], P('seq', 'cfg')
- denoised: float32 [192, 64], P('seq', 'cfg')
Inputs may be any that keep to these rules, and one draw needn't show every extreme that they name: `query_gain`: gains are positive. `key_gain`: gains are positive. `text_gain`: gains are positive. `text_lengths`: one of the two halves has all 16 slots within its length.
All inputs are finite; a program needn't handle non-finite values.
Results may differ from a plain program's by a relative error of at most 0.007.
The roundings to bfloat16 on the way count: a program that leaves them out, or rounds other values in their place, can miss the bound.
Values may be sent and summed in bfloat16 or wider, within the bound.
A program may use at most 128 MiB of HBM per device.

v0:
```python
import math

import jax
import jax.numpy as jnp
from jax import lax
from jax.sharding import PartitionSpec as P

STEPS = 28


epsilon = 1e-06
guidance = 3.5
shift_factor = 3.0
masked_score = -1e30


def from_partner(block, axis, stride):
    count = lax.axis_size(axis)
    route = []
    for low in range(count):
        high = low | 1 << stride
        if high != low and high < count:
            route += [(low, high), (high, low)]
    return lax.ppermute(block, axis, route)


def head_norm(values, gain_row):
    widened = values.astype(jnp.float32).reshape(values.shape[0], -1, gain_row.shape[0])
    scaled = (
        widened
        * lax.rsqrt(jnp.mean(widened * widened, axis=-1, keepdims=True) + epsilon)
        * gain_row
    )
    return scaled.astype(jnp.bfloat16)


def sigma_at(position):
    time_left = 1.0 - position / STEPS
    return shift_factor * time_left / (1.0 + (shift_factor - 1.0) * time_left)


def attend_block(running, queries, keys_block, values_block, usable):
    run_max, run_total, run_sum = running
    head_count = queries.shape[1]
    head_size = queries.shape[2]
    keys_heads = keys_block.reshape(keys_block.shape[0], head_count, head_size)
    values_heads = values_block.reshape(values_block.shape[0], head_count, head_size)
    scores = jnp.einsum("rhd,khd->hrk", queries, keys_heads, preferred_element_type=jnp.float32) * (
        1.0 / math.sqrt(head_size)
    )
    scores = jnp.where(usable[None, None, :], scores, masked_score)
    new_max = jnp.maximum(run_max, jnp.max(scores, axis=-1))
    factor = jnp.exp(run_max - new_max)
    weights_block = jnp.where(usable[None, None, :], jnp.exp(scores - new_max[..., None]), 0.0)
    run_total = run_total * factor + jnp.sum(weights_block, axis=-1)
    run_sum = run_sum * factor[..., None] + jnp.einsum(
        "hrk,khd->hrd",
        weights_block.astype(jnp.bfloat16),
        values_heads,
        preferred_element_type=jnp.float32,
    )
    return (new_max, run_total, run_sum)


def attend_text(running, queries, keys_block, values_block, usable_flags):
    usable = usable_flags == 1

    def take_block(state_in):
        return attend_block(state_in, queries, keys_block, values_block, usable)

    def keep_state(state_in):
        return state_in

    return lax.cond(jnp.any(usable), take_block, keep_state, running)


def on_device(
    img_queries,
    img_keys,
    img_values,
    text_keys,
    text_values,
    query_gain,
    key_gain,
    text_gain,
    text_lengths,
    text_blocks,
    latent,
    base_velocity,
    out_weight,
    timestep,
):
    head_size = query_gain.shape[0]
    head_count = img_queries.shape[2] // head_size
    row_count = img_queries.shape[1]
    text_count = text_keys.shape[1]
    queries = head_norm(img_queries[0], query_gain)
    keys_local = head_norm(img_keys[0], key_gain).reshape(row_count, head_count * head_size)
    values_local = img_values[0]
    text_keys_local = head_norm(text_keys[0], text_gain).reshape(text_count, head_count * head_size)
    text_values_local = text_values[0]
    slot_index = lax.axis_index("seq") * text_count + jnp.arange(text_count, dtype=jnp.int32)
    usable_text = ((slot_index < text_lengths[0]) & (text_blocks[0, 0] == 1)).astype(jnp.int32)
    initial = (
        jnp.full((head_count, row_count), masked_score, jnp.float32),
        jnp.zeros((head_count, row_count), jnp.float32),
        jnp.zeros((head_count, row_count, head_size), jnp.float32),
    )
    running = initial
    key_piece = lax.all_gather(keys_local, "seq", axis=0, tiled=True)
    value_piece = lax.all_gather(values_local, "seq", axis=0, tiled=True)
    text_key_piece = lax.all_gather(text_keys_local, "seq", axis=0, tiled=True)
    text_value_piece = lax.all_gather(text_values_local, "seq", axis=0, tiled=True)
    usable_piece = lax.all_gather(usable_text, "seq", axis=0, tiled=True)
    every_key = jnp.ones((key_piece.shape[0],), dtype=jnp.bool_)
    running = attend_block(running, queries, key_piece, value_piece, every_key)
    final_state = attend_text(running, queries, text_key_piece, text_value_piece, usable_piece)
    run_max, run_total, run_sum = final_state
    attended = (
        (run_sum / run_total[..., None])
        .transpose(1, 0, 2)
        .reshape(row_count, head_count * head_size)
        .astype(jnp.bfloat16)
    )
    velocity = base_velocity[0].astype(jnp.float32) + jnp.dot(
        attended, out_weight, preferred_element_type=jnp.float32
    )
    guide_half = lax.axis_index("cfg")
    half_width = latent.shape[1]
    own_part = lax.dynamic_slice_in_dim(velocity, guide_half * half_width, half_width, 1)
    sent_part = lax.dynamic_slice_in_dim(velocity, (1 - guide_half) * half_width, half_width, 1)
    partner = from_partner(sent_part, "cfg", 0)
    cond_part = jnp.where(guide_half == 0, own_part, partner)
    uncond_part = jnp.where(guide_half == 0, partner, own_part)
    guided = uncond_part + guidance * (cond_part - uncond_part)
    step_now = timestep[0].astype(jnp.float32)
    sigma_now = sigma_at(step_now)
    sigma_next = sigma_at(step_now + 1.0)
    next_latent = latent + (sigma_next - sigma_now) * guided
    denoised = latent - sigma_now * guided
    return (next_latent, denoised)


def solution(mesh):
    return jax.shard_map(
        on_device,
        mesh=mesh,
        in_specs=(
            P("cfg", "seq", None),
            P("cfg", "seq", None),
            P("cfg", "seq", None),
            P("cfg", "seq", None),
            P("cfg", "seq", None),
            P(),
            P(),
            P(),
            P("cfg"),
            P("cfg", "seq"),
            P("seq", "cfg"),
            P("cfg", "seq", None),
            P(),
            P(),
        ),
        out_specs=(P("seq", "cfg"), P("seq", "cfg")),
        check_vma=False,
    )
```

profile of v0, /device:TPU:0, one launch (start us, length us, event | category | flops | bytes accessed | tf_op | source)
XLA Modules:
  0.0 111.0 jit_solution(14130613477669451917)
XLA Ops:
  0.7 0.9 reshape.183
  1.7 0.8 convert_multiply_fusion
  3.1 25.1 %all-gather.2 = bf16[16,12,1216]{2,1,0:T(8,128)(2,1)S(1)} all-gather(bf16[1,12,1216]{2,1,0:T(8,128)(2,1)S(1)} %fusion.21), channel_id=1, replica_groups=mesh['cfg'=2,'seq'=16] {'seq'}, dimensions={0}, use_global_device_ids=true | all-gather | bytes 496128 | tf_op jit(solution)/shard_map/all_gather | solution.py:110
  28.2 0.8 reshape.174
  29.1 0.7 fusion.31
  29.8 0.2 fusion.13
  30.1 20.3 %all-gather = bf16[1,192,1216]{2,0,1:T(2,128)(2,1)S(1)} all-gather(bf16[1,12,1216]{2,0,1:T(2,128)(2,1)S(1)} %copy.42), channel_id=2, replica_groups=mesh['cfg'=2,'seq'=16] {'seq'}, dimensions={1}, use_global_device_ids=true | all-gather | bytes 496128 | tf_op jit(solution)/shard_map/all_gather | solution.py:111
  51.7 0.6 dynamic-slice
  52.3 0.7 fusion.27
  53.1 1.3 %copy.43 = bf16[1,192,1216]{1,2,0:T(8,128)(2,1)S(1)} copy(bf16[1,192,1216]{2,0,1:T(2,128)(2,1)S(1)} %all-gather) | data formatting | bytes 933888 | tf_op jit(solution)/shard_map/all_gather | solution.py:111
  54.4 9.6 %all-reduce = s32[16]{0:T(128)S(1)} all-reduce(s32[16]{0:T(128)S(1)} %fusion.27), channel_id=1, replica_groups=mesh['cfg'=2,'seq'=16] {'seq'}, use_global_device_ids=true, to_apply=%add | all-reduce | flops 16 | bytes 128
  64.0 0.6 broadcast_compare_fusion
  65.1 20.9 %all-gather.3 = bf16[16,1,1216]{2,1,0:T(2,128)(2,1)S(1)} all-gather(bf16[1,1,1216]{2,1,0:T(2,128)(2,1)S(1)} %fusion.24), channel_id=1, replica_groups=mesh['cfg'=2,'seq'=16] {'seq'}, dimensions={0}, use_global_device_ids=true | all-gather | bytes 41344 | tf_op jit(solution)/shard_map/all_gather | solution.py:112
  86.0 17.6 %all-gather.1 = bf16[16,1,1216]{2,1,0:T(2,128)(2,1)S(1)} all-gather(bf16[1,1,1216]{2,1,0:T(2,128)(2,1)S(1)} %copy-done.5), channel_id=3, replica_groups=mesh['cfg'=2,'seq'=16] {'seq'}, dimensions={0}, use_global_device_ids=true | all-gather | bytes 41344 | tf_op jit(solution)/shard_map/all_gather | solution.py:113
  104.3 0.3 convolution_add_fusion.1
  104.7 1.5 %conditional.1 = ((f32[19,12]{1,0:T(8,128)S(1)}, f32[19,12,64]{2,1,0:T(8,128)S(1)})) conditional(s32[]{:T(128)} %convert_element_type.112, (f32[19,12]{1,0:T(8,128)S(1)}, f32[19,12,64]{2,1,0:T(8,128)S(1)}) %tuple.15, (pred[16]{0:T(512)(128)(4,1)S(1)}, bf16[16,1,1216]{2,1,0:T(2,128)(2,1)S(1)}, bf16[12,19,64]{2,1,0:T(8,128)(2,1)S(1)}, ...), branch_computations={%region_6.7_spmd, %region_7.10_spmd} | conditional | flops 996360 | bytes 591660 | solution.py:74
  104.7 0.2 reduce.2
  105.0 0.2 fusion.30
  105.3 0.2 fusion.2
  105.5 0.2 reduce.3
  105.9 0.3 convolution_add_fusion
  106.7 1.5 %collective-permute-start = (f32[12,32]{1,0:T(8,128)S(1)}, f32[12,32]{1,0:T(8,128)S(1)}, u32[]{:S(2)}, u32[]{:S(2)}) collective-permute-start(f32[12,32]{1,0:T(8,128)S(1)} %constant_dynamic-slice_fusion), channel_id=1, source_target_pairs={{0,16},{16,0},{1,17},{17,1},{2,18},{18,2},{3,19},{19,3},{4,20},{20... | collective-permute-start | bytes 4616 | tf_op jit(solution)/shard_map/ppermute | solution.py:24
  108.9 1.4 %collective-permute-done = f32[12,32]{1,0:T(8,128)S(1)} collective-permute-done((f32[12,32]{1,0:T(8,128)S(1)}, f32[12,32]{1,0:T(8,128)S(1)}, u32[]{:S(2)}, u32[]{:S(2)}) %collective-permute-start) | collective-permute-done | bytes 1568 | tf_op jit(solution)/shard_map/ppermute | solution.py:24
  110.4 0.7 multiply_subtract_fusion
  (55 shorter events, 2.0 us)
Async XLA Ops:
  0.6 105.8 %copy-start = (bf16[1216,64]{0,1:T(8,128)(2,1)S(1)}, bf16[1216,64]{0,1:T(8,128)(2,1)}, u32[]{:S(2)}) copy-start(bf16[1216,64]{0,1:T(8,128)(2,1)} %param.28) | copy-start | bytes 466948
  0.6 2.4 %copy-start.1 = (bf16[1,12,1216]{2,1,0:T(8,128)(2,1)S(1)}, bf16[1,12,1216]{2,1,0:T(8,128)(2,1)}, u32[]{:S(2)}) copy-start(bf16[1,12,1216]{2,1,0:T(8,128)(2,1)} %param.17) | copy-start | bytes 87556
  0.7 2.3 %copy-start.8 = (f32[64]{0:T(128)S(1)}, f32[64]{0:T(128)}, u32[]{:S(2)}) copy-start(f32[64]{0:T(128)} %param.22) | copy-start | bytes 772
  3.0 25.9 %copy-start.7 = (f32[64]{0:T(128)S(1)}, f32[64]{0:T(128)}, u32[]{:S(2)}) copy-start(f32[64]{0:T(128)} %param.21) | copy-start | bytes 772
  29.0 1.1 copy-start.2
  29.1 22.6 %copy-start.10 = (u32[32]{0:T(128)S(1)}, u32[32]{0:T(128)}, u32[]{:S(2)}) copy-start(u32[32]{0:T(128)} %constant.88) | copy-start | bytes 388
  30.1 34.5 %copy-start.3 = (bf16[1,1,1216]{2,1,0:T(2,128)(2,1)S(1)}, bf16[1,1,1216]{2,1,0:T(2,128)(2,1)}, u32[]{:S(2)}) copy-start(bf16[1,1,1216]{2,1,0:T(2,128)(2,1)} %param.19) | copy-start | bytes 7300
  30.1 34.9 %copy-start.9 = (f32[64]{0:T(128)S(1)}, f32[64]{0:T(128)}, u32[]{:S(2)}) copy-start(f32[64]{0:T(128)} %param.23) | copy-start | bytes 772
  50.4 35.6 %copy-start.5 = (bf16[1,1,1216]{2,1,0:T(2,128)(2,1)S(1)}, bf16[1,1,1216]{2,1,0:T(2,128)(2,1)}, u32[]{:S(2)}) copy-start(bf16[1,1,1216]{2,1,0:T(2,128)(2,1)} %param.20) | copy-start | bytes 7300
  104.6 1.8 %copy-start.6 = (bf16[1,12,64]{2,1,0:T(8,128)(2,1)S(1)}, bf16[1,12,64]{2,1,0:T(8,128)(2,1)}, u32[]{:S(2)}) copy-start(bf16[1,12,64]{2,1,0:T(8,128)(2,1)} %param.27) | copy-start | bytes 4612
  104.6 5.7 %copy-start.4 = (f32[12,32]{1,0:T(8,128)S(1)}, f32[12,32]{1,0:T(8,128)}, u32[]{:S(2)}) copy-start(f32[12,32]{1,0:T(8,128)} %param.26) | copy-start | bytes 4612
  106.7 3.7 %collective-permute-start = (f32[12,32]{1,0:T(8,128)S(1)}, f32[12,32]{1,0:T(8,128)S(1)}, u32[]{:S(2)}, u32[]{:S(2)}) collective-permute-start(f32[12,32]{1,0:T(8,128)S(1)} %constant_dynamic-slice_fusion), channel_id=1, source_target_pairs={{0,16},{16,0},{1,17},{17,1},{2,18},{18,2},{3,19},{19,3},{4,20},{20... | collective-permute-start | bytes 4616 | tf_op jit(solution)/shard_map/ppermute | solution.py:24
where the time goes:
time: 111 us
  blocking collectives  93.5 us (84%)
  local copies, waits for them, and re-layouts  4.8 us (4%)
  other arithmetic  4.41 us (4%)
  between operations  3.63 us (3%)
  matrix products  1.67 us (2%)
  starting transfers between devices  1.51 us (1%)
  waiting for transfers between devices  1.42 us (1%)
    all_gather x1, blocking collectives, on_device(): key_piece = lax.all_gather(keys_local, 'seq', axis=0, tiled=True)  25.1 us
    all_gather x1, blocking collectives, on_device(): text_key_piece = lax.all_gather(text_keys_local, 'seq', axis=0, tiled=True)  20.9 us
    all_gather x1, blocking collectives, on_device(): value_piece = lax.all_gather(values_local, 'seq', axis=0, tiled=True)  20.3 us
    all_gather x1, blocking collectives, on_device(): lax.all_gather(text_values_local, 'seq', axis=0, tiled=True)  17.6 us
    unnamed x1, blocking collectives  9.61 us
  transfers between devices with their start and end apart: 1, of which 1 were waited for; matrix products, arithmetic and copies ran while one was open for 0% of the time, Pallas kernels for 0%

commit v1 on v0

v1 whole, which is shorter than its diff:
```python
import functools
import math

import jax
import jax.numpy as jnp
from jax import lax
from jax.experimental import pallas as pl
from jax.experimental.pallas import tpu as pltpu
from jax.sharding import PartitionSpec as P

STEPS = 28
MESH = pl.DeviceIdType.MESH

epsilon = 1e-06
guidance = 3.5
shift_factor = 3.0
masked_score = -1e30

SLOT_ROWS = 16
PACK = 4


def sigma_at(position):
    time_left = 1.0 - position / STEPS
    return shift_factor * time_left / (1.0 + (shift_factor - 1.0) * time_left)


def exchange_kernel(
    plan,
    q_hbm, k_hbm, v_hbm, tk_hbm, tv_hbm, gq_ref, gk_ref, gt_ref, len_ref, blk_ref, base_hbm, w_hbm,
    out_ref,
    q_in, k_in, v_in, tk_in, tv_in, base_in, w_in,
    stage, recv, packed, wide, parts, recv2,
    load_sem, send_sem, recv_sem, send2_sem, recv2_sem,
):
    n, group, heads, head_size, rows, texts, half = plan
    extras = heads - group
    f32, bf16 = jnp.float32, jnp.bfloat16
    cfg = lax.axis_index("cfg")
    me = lax.axis_index("seq")
    place = lax.rem(me, group)
    first = me - place
    row_groups = rows // PACK

    def extra_of(position):
        step = position - group // 4
        index = lax.div(step, 3)
        has = (step >= 0) & (lax.rem(step, 3) == 0) & (index < extras)
        return has, group + jnp.clip(index, 0, extras - 1)

    has_extra, extra_head = extra_of(place)

    loads = []
    sources = (
        (k_hbm.at[0], k_in), (tk_hbm.at[0], tk_in), (q_hbm.at[0], q_in), (v_hbm.at[0], v_in), (tv_hbm.at[0], tv_in),
        (base_hbm.at[0], base_in),
        (w_hbm.at[pl.ds(pl.multiple_of(place * head_size, head_size), head_size)], w_in.at[0]),
        (w_hbm.at[pl.ds(pl.multiple_of(extra_head * head_size, head_size), head_size)], w_in.at[1]),
    )
    for i, (src, dst) in enumerate(sources):
        load = pltpu.make_async_copy(src, dst, load_sem.at[i])
        load.start()
        loads.append(load)

    barrier = pltpu.get_barrier_semaphore()

    def greet_half(i, carry):
        peer = lax.rem(me + i, n)
        pl.semaphore_signal(barrier, inc=1, device_id=(cfg, peer), device_id_type=MESH)
        return carry

    def greet_other(i, carry):
        pl.semaphore_signal(barrier, inc=1, device_id=(1 - cfg, first + i), device_id_type=MESH)
        return carry

    lax.fori_loop(1, n, greet_half, 0)
    lax.fori_loop(0, group, greet_other, 0)

    lane = lax.broadcasted_iota(jnp.int32, (SLOT_ROWS, 128), 1)
    row = lax.broadcasted_iota(jnp.int32, (SLOT_ROWS, 128), 0)
    low = lane < head_size
    gain_q = jnp.concatenate([gq_ref[...], gq_ref[...]], axis=1) * (1.0 / math.sqrt(head_size))
    gain_k = jnp.concatenate([gk_ref[...], gk_ref[...]], axis=1)
    gain_t = jnp.concatenate([gt_ref[...], gt_ref[...]], axis=1)
    is_text = (row >= rows) & (row < rows + texts)
    gain_kt = jnp.where(is_text, gain_t, gain_k)
    slot_index = me * texts + row - rows
    open_row = (row < rows) | (is_text & (slot_index < len_ref[0]) & (blk_ref[0, 0] == 1))
    bias = jnp.where((lane == 0) & jnp.logical_not(open_row), masked_score, 0.0)

    def chunk(ref, c):
        part = ref[:, c * 128:min((c + 1) * 128, heads * head_size)].astype(f32)
        if part.shape[1] < 128:
            part = jnp.concatenate([part, jnp.zeros((part.shape[0], 128 - part.shape[1]), f32)], axis=1)
        return part

    def tall(part):
        return jnp.concatenate([part, jnp.zeros((SLOT_ROWS - part.shape[0], 128), f32)], axis=0)

    def with_text(part, text):
        if texts == 1:
            return jnp.where(row == rows, text, tall(part))
        return tall(jnp.concatenate([part, text], axis=0))

    def normed(part, gain):
        square = part * part
        left = jnp.sum(jnp.where(low, square, 0.0), axis=1, keepdims=True)
        right = jnp.sum(jnp.where(low, 0.0, square), axis=1, keepdims=True)
        mean = jnp.where(low, left, right) * (1.0 / head_size)
        return part * lax.rsqrt(mean + epsilon) * gain

    for load in loads[:5]:
        load.wait()
    for c in range((heads + 1) // 2):
        qn = normed(tall(chunk(q_in, c)), gain_q)
        kn = normed(with_text(chunk(k_in, c), chunk(tk_in, c)), gain_kt)
        vv = with_text(chunk(v_in, c), chunk(tv_in, c))
        q_turn = pltpu.roll(qn, head_size, 1)
        k_turn = pltpu.roll(kn, head_size, 1)
        v_turn = pltpu.roll(vv, head_size, 1)
        stage[2 * c, :, 0:128] = jnp.where(low, bias, k_turn).astype(bf16)
        stage[2 * c, :, 128:256] = jnp.where(low, vv, q_turn).astype(bf16)
        if 2 * c + 1 < heads:
            stage[2 * c + 1, :, 0:128] = jnp.where(low, bias, kn).astype(bf16)
            stage[2 * c + 1, :, 128:256] = jnp.where(low, v_turn, qn).astype(bf16)

    pl.semaphore_wait(barrier, n - 1 + group)

    def head_copy(peer, slot, head):
        return pltpu.make_async_remote_copy(
            src_ref=stage.at[head],
            dst_ref=recv.at[slot, me],
            send_sem=send_sem.at[slot, peer],
            recv_sem=recv_sem.at[slot],
            device_id=(cfg, peer),
            device_id_type=MESH,
        )

    def send_heads(i, carry):
        peer = lax.rem(me + i, n)
        position = lax.rem(peer, group)
        more, more_head = extra_of(position)

        @pl.when(more)
        def _():
            head_copy(peer, 1, more_head).start()

        head_copy(peer, 0, position).start()
        return carry

    lax.fori_loop(1, n, send_heads, 0)
    recv[0, me] = stage[place]

    @pl.when(has_extra)
    def _():
        recv[1, me] = stage[extra_head]

    for load in loads[5:]:
        load.wait()
    lane_w = lax.broadcasted_iota(jnp.int32, (head_size, 128), 1)
    for slot in range(2):
        weight = w_in[slot].astype(f32)
        for side in range(2):
            block = weight[:, side * half:(side + 1) * half]
            tiled = jnp.concatenate([block] * (128 // half), axis=1)
            for g in range(row_groups):
                held = jnp.where(lax.div(lane_w, half) == g, tiled, 0.0)
                wide[slot, g, 0:head_size, side * 128:(side + 1) * 128] = held.astype(bf16)
                wide[slot, g, head_size:128, side * 128:(side + 1) * 128] = jnp.zeros((128 - head_size, 128), bf16)
    base = base_in[...].astype(f32)
    base_packed = []
    for side in range(2):
        pieces = [base[g * PACK:(g + 1) * PACK, side * half:(side + 1) * half] for g in range(row_groups)]
        pieces.append(jnp.zeros((PACK, 128 - row_groups * half), f32))
        base_packed.append(jnp.concatenate(pieces, axis=1))

    lane_q = lax.broadcasted_iota(jnp.int32, (group * PACK, 128), 1)

    def whole_wait(buffer, count, sem):
        span = buffer.at[pl.ds(0, count)]
        pltpu.make_async_copy(span, span, sem).wait()

    def attend(slot):
        whole_wait(recv.at[slot], n - 1, recv_sem.at[slot])
        keys = recv[slot, :, :, 0:128].reshape(n * SLOT_ROWS, 128)
        values = recv[slot, :, :, 128:256].reshape(n * SLOT_ROWS, 128)
        for s in range(group):
            own = recv[slot, first + s, :, 128:256].astype(f32)
            for g in range(row_groups):
                packed[g, s * PACK:(s + 1) * PACK, :] = own[g * PACK:(g + 1) * PACK]
        total = None
        for g in range(row_groups):
            query = jnp.where(lane_q < head_size, jnp.where(lane_q == 0, 1.0, 0.0), packed[g]).astype(bf16)
            scores = lax.dot_general(query, keys, (((1,), (1,)), ((), ())), preferred_element_type=f32)
            top = jnp.max(scores, axis=1, keepdims=True)
            weights = jnp.exp(scores - top)
            den = jnp.sum(weights, axis=1, keepdims=True)
            num = jnp.dot(weights.astype(bf16), values, preferred_element_type=f32)
            attended = (num / den).astype(bf16)
            term = jnp.dot(attended, wide[slot, g], preferred_element_type=f32)
            total = term if total is None else total + term
        return total

    total = attend(0)
    for side in range(2):
        for s in range(group):
            parts[side, s] = total[s * PACK:(s + 1) * PACK, side * 128:(side + 1) * 128]

    @pl.when(has_extra)
    def _():
        more_total = attend(1)
        for side in range(2):
            for s in range(group):
                parts[side, s] = parts[side, s] + more_total[s * PACK:(s + 1) * PACK, side * 128:(side + 1) * 128]

    for side in range(2):
        parts[side, place] = parts[side, place] + base_packed[side]

    mine = cfg * group + place

    def part_copy(side, s):
        return pltpu.make_async_remote_copy(
            src_ref=parts.at[side, s],
            dst_ref=recv2.at[mine],
            send_sem=send2_sem.at[side * group + s],
            recv_sem=recv2_sem,
            device_id=(side, first + s),
            device_id_type=MESH,
        )

    def send_parts(i, carry):
        target = lax.rem(mine + i, 2 * group)
        part_copy(lax.div(target, group), lax.rem(target, group)).start()
        return carry

    lax.fori_loop(1, 2 * group, send_parts, 0)
    recv2[mine] = parts[cfg, place]

    def sent_heads(i, carry):
        peer = lax.rem(me + i, n)
        more, more_head = extra_of(lax.rem(peer, group))

        @pl.when(more)
        def _():
            head_copy(peer, 1, more_head).wait_send()

        head_copy(peer, 0, lax.rem(peer, group)).wait_send()
        return carry

    lax.fori_loop(1, n, sent_heads, 0)

    whole_wait(recv2, 2 * group - 1, recv2_sem)
    cond = jnp.sum(recv2[0:group], axis=0)
    uncond = jnp.sum(recv2[group:2 * group], axis=0)
    guided = uncond + guidance * (cond - uncond)
    for g in range(row_groups):
        out_ref[g * PACK:(g + 1) * PACK, :] = guided[:, g * half:(g + 1) * half]

    def sent_parts(i, carry):
        target = lax.rem(mine + i, 2 * group)
        part_copy(lax.div(target, group), lax.rem(target, group)).wait_send()
        return carry

    lax.fori_loop(1, 2 * group, sent_parts, 0)


def on_device(
    n,
    img_queries, img_keys, img_values, text_keys, text_values, query_gain, key_gain, text_gain,
    text_lengths, text_blocks, latent, base_velocity, out_weight, timestep,
):
    head_size = query_gain.shape[0]
    width = img_queries.shape[2]
    heads = width // head_size
    rows, texts = img_queries.shape[1], text_keys.shape[1]
    half = latent.shape[1]
    group = max(d for d in range(1, min(n, heads) + 1) if n % d == 0)
    plan = (n, group, heads, head_size, rows, texts, half)
    bf16, f32 = jnp.bfloat16, jnp.float32
    anywhere = pl.BlockSpec(memory_space=pl.ANY)
    vmem = pl.BlockSpec(memory_space=pltpu.VMEM)
    smem = pl.BlockSpec(memory_space=pltpu.SMEM)
    guided = pl.pallas_call(
        functools.partial(exchange_kernel, plan),
        out_shape=jax.ShapeDtypeStruct((rows, half), f32),
        in_specs=[anywhere] * 5 + [vmem] * 3 + [smem] * 2 + [anywhere] * 2,
        out_specs=vmem,
        scratch_shapes=[
            pltpu.VMEM((rows, width), bf16),
            pltpu.VMEM((rows, width), bf16),
            pltpu.VMEM((rows, width), bf16),
            pltpu.VMEM((texts, width), bf16),
            pltpu.VMEM((texts, width), bf16),
            pltpu.VMEM((rows, 2 * half), bf16),
            pltpu.VMEM((2, head_size, 2 * half), bf16),
            pltpu.VMEM((heads, SLOT_ROWS, 256), bf16),
            pltpu.VMEM((2, n, SLOT_ROWS, 256), bf16),
            pltpu.VMEM((rows // PACK, group * PACK, 128), f32),
            pltpu.VMEM((2, rows // PACK, 128, 256), bf16),
            pltpu.VMEM((2, group, PACK, 128), f32),
            pltpu.VMEM((2 * group, PACK, 128), f32),
            pltpu.SemaphoreType.DMA((8,)),
            pltpu.SemaphoreType.DMA((2, n)),
            pltpu.SemaphoreType.DMA((2,)),
            pltpu.SemaphoreType.DMA((2 * group,)),
            pltpu.SemaphoreType.DMA,
        ],
        compiler_params=pltpu.CompilerParams(
            collective_id=0, has_side_effects=True, vmem_limit_bytes=40 * 1024 * 1024
        ),
    )(
        img_queries, img_keys, img_values, text_keys, text_values,
        query_gain.reshape(1, -1), key_gain.reshape(1, -1), text_gain.reshape(1, -1),
        text_lengths, text_blocks, base_velocity, out_weight,
    )
    step_now = timestep[0].astype(f32)
    sigma_now = sigma_at(step_now)
    sigma_next = sigma_at(step_now + 1.0)
    next_latent = latent + (sigma_next - sigma_now) * guided
    denoised = latent - sigma_now * guided
    return (next_latent, denoised)


def solution(mesh):
    return jax.shard_map(
        functools.partial(on_device, mesh.shape["seq"]),
        mesh=mesh,
        in_specs=(
            P("cfg", "seq", None),
            P("cfg", "seq", None),
            P("cfg", "seq", None),
            P("cfg", "seq", None),
            P("cfg", "seq", None),
            P(),
            P(),
            P(),
            P("cfg"),
            P("cfg", "seq"),
            P("seq", "cfg"),
            P("cfg", "seq", None),
            P(),
            P(),
        ),
        out_specs=(P("seq", "cfg"), P("seq", "cfg")),
        check_vma=False,
    )
```

time: 111 us -> 25 us (0.23)
  blocking collectives: 93.5 us -> 0 us
  Pallas kernels: 0 us -> 19.5 us
  other arithmetic: 4.41 us -> 0.61 us
  local copies, waits for them, and re-layouts: 4.8 us -> 1.88 us
  matrix products: 1.67 us -> 0 us
  starting transfers between devices: 1.51 us -> 0 us
  waiting for transfers between devices: 1.42 us -> 0 us
    all_gather x4 -> x0, blocking collectives: 83.9 us -> none  [the longest x1 25.1 us: on_device(): key_piece = lax.all_gather(keys_local, 'seq', axis=0, tiled=True)]
    pallas_call x0 -> x1, Pallas kernels: none -> 19.5 us  [on_device(): pl.pallas_call(functools.partial(exchange_kernel, plan), out_shape=jax.Sh...]
    unnamed x1 -> x0, blocking collectives: 9.61 us -> none
    dot_general x5 -> x0, matrix products: 1.67 us -> none  [the longest x2 0.91 us: attend_block(): jnp.einsum('rhd,khd->hrk', queries, keys_heads, preferred_element_type=jn...]
    ppermute x1 -> x0, starting transfers between devices: 1.51 us -> none  [from_partner(): return lax.ppermute(block, axis, route)]
    ppermute x1 -> x0, waiting for transfers between devices: 1.42 us -> none  [from_partner(): return lax.ppermute(block, axis, route)]
    all_gather x1 -> x0, local copies, waits for them, and re-layouts: 1.3 us -> none  [on_device(): value_piece = lax.all_gather(values_local, 'seq', axis=0, tiled=True)]
    unnamed x25 -> x21, local copies, waits for them, and re-layouts: 0.7 us -> 1.88 us
  transfers between devices with their start and end apart: 1 -> 0, of which waited for: 1 -> 0; matrix products, arithmetic and copies ran while one was open for 0% -> 0% of each run, Pallas kernels for 0% -> 0%
where the time goes in v1:
time: 25 us; the launch traced here: 24.8 us
  Pallas kernels  19.5 us (78%)
  between operations  2.82 us (11%)
  local copies, waits for them, and re-layouts  1.88 us (8%)
  other arithmetic  0.61 us (2%)
    pallas_call x1, Pallas kernels, on_device(): pl.pallas_call(functools.partial(exchange_kernel, plan), out_shape=jax.Sh...  19.5 us
    unnamed x21, local copies, waits for them, and re-layouts  1.88 us
    sub x1, other arithmetic, on_device(): denoised = latent - sigma_now * guided  0.61 us

profile of v1, /device:TPU:0, one launch (start us, length us, event | category | flops | bytes accessed | tf_op | source)
XLA Modules:
  0.0 24.8 jit_solution(13039869532386737352)
XLA Ops:
  1.9 0.0 copy-start
  1.9 0.0 copy-start.1
  1.9 0.0 copy-start.2
  2.0 0.0 copy-start.3
  2.0 0.0 copy-start.4
  2.0 0.0 copy-start.5
  2.0 0.0 copy-start.6
  2.0 0.0 copy-start.7
  2.0 0.0 copy-start.8
  2.0 1.2 %copy.16.w_hbm = bf16[1216,64]{1,0:T(8,128)(2,1)S(1)} copy(bf16[1216,64]{0,1:T(8,128)(2,1)} %param.26) | data formatting | bytes 311296 | tf_op args[12]
  3.2 0.0 copy-done
  3.2 0.0 copy-done.1
  3.2 0.0 copy-done.2
  3.2 0.0 copy-done.3
  3.2 0.0 copy-done.4
  3.3 0.0 copy-done.5
  3.3 0.0 copy-done.6
  3.3 0.0 copy-done.7
  3.3 0.0 copy-done.8
  3.3 19.5 %shard_map.149 = f32[12,32]{1,0:T(8,128)S(1)} custom-call(bf16[1,12,1216]{2,1,0:T(8,128)(2,1)S(1)} %copy-done, bf16[1,12,1216]{2,1,0:T(8,128)(2,1)S(1)} %copy-done.1, bf16[1,12,1216]{2,1,0:T(8,128)(2,1)S(1)} %copy-done.2, bf16[1,1,1216]{2,1,0:T(2,128)(2,1)S(1)} %copy-done.3, bf16[1,1,1216]{2,1,0:T(2,128)(2,1)S(1)} %copy-done.4, f32[1,64]{1,0:T(1,128)S(1)} %bitcast.5, ...), custom_call_target="tpu_custom_call" | custom-call | tf_op jit(solution)/shard_map/pallas_call | solution.py:283
  23.5 0.0 copy-start.9
  23.5 0.6 %copy-done.9 = f32[12,32]{1,0:T(8,128)S(1)} copy-done((f32[12,32]{1,0:T(8,128)S(1)}, f32[12,32]{1,0:T(8,128)}, u32[]{:S(2)}) %copy-start.9) | copy-done | bytes 1560
  24.2 0.6 %multiply_subtract_fusion = (f32[12,32]{1,0:T(8,128)}, f32[12,32]{1,0:T(8,128)}) fusion(f32[12,32]{1,0:T(8,128)S(1)} %copy-done.9, f32[12,32]{1,0:T(8,128)S(1)} %shard_map.149, f32[]{:T(128)} %bitcast.1, f32[]{:T(128)S(6)} %sub.19), kind=kLoop, calls=%fused_computation | loop fusion | flops 1536 | bytes 6152 | tf_op jit(solution)/shard_map/sub | solution.py:320
Async XLA Ops:
  1.9 1.3 %copy-start = (bf16[1,12,1216]{2,1,0:T(8,128)(2,1)S(1)}, bf16[1,12,1216]{2,1,0:T(8,128)(2,1)}, u32[]{:S(2)}) copy-start(bf16[1,12,1216]{2,1,0:T(8,128)(2,1)} %q_hbm.1) | copy-start | bytes 87556
  1.9 1.3 %copy-start.1 = (bf16[1,12,1216]{2,1,0:T(8,128)(2,1)S(1)}, bf16[1,12,1216]{2,1,0:T(8,128)(2,1)}, u32[]{:S(2)}) copy-start(bf16[1,12,1216]{2,1,0:T(8,128)(2,1)} %k_hbm.1) | copy-start | bytes 87556
  1.9 1.3 %copy-start.2 = (bf16[1,12,1216]{2,1,0:T(8,128)(2,1)S(1)}, bf16[1,12,1216]{2,1,0:T(8,128)(2,1)}, u32[]{:S(2)}) copy-start(bf16[1,12,1216]{2,1,0:T(8,128)(2,1)} %v_hbm.1) | copy-start | bytes 87556
  2.0 1.3 %copy-start.3 = (bf16[1,1,1216]{2,1,0:T(2,128)(2,1)S(1)}, bf16[1,1,1216]{2,1,0:T(2,128)(2,1)}, u32[]{:S(2)}) copy-start(bf16[1,1,1216]{2,1,0:T(2,128)(2,1)} %tk_hbm.1) | copy-start | bytes 7300
  2.0 1.3 %copy-start.4 = (bf16[1,1,1216]{2,1,0:T(2,128)(2,1)S(1)}, bf16[1,1,1216]{2,1,0:T(2,128)(2,1)}, u32[]{:S(2)}) copy-start(bf16[1,1,1216]{2,1,0:T(2,128)(2,1)} %tv_hbm.1) | copy-start | bytes 7300
  2.0 1.3 %copy-start.5 = (bf16[1,12,64]{2,1,0:T(8,128)(2,1)S(1)}, bf16[1,12,64]{2,1,0:T(8,128)(2,1)}, u32[]{:S(2)}) copy-start(bf16[1,12,64]{2,1,0:T(8,128)(2,1)} %base_hbm.1) | copy-start | bytes 4612
  2.0 1.3 %copy-start.6 = (f32[64]{0:T(128)S(1)}, f32[64]{0:T(128)}, u32[]{:S(2)}) copy-start(f32[64]{0:T(128)} %param.19) | copy-start | bytes 772
  2.0 1.3 %copy-start.7 = (f32[64]{0:T(128)S(1)}, f32[64]{0:T(128)}, u32[]{:S(2)}) copy-start(f32[64]{0:T(128)} %param.20) | copy-start | bytes 772
  2.0 1.3 %copy-start.8 = (f32[64]{0:T(128)S(1)}, f32[64]{0:T(128)}, u32[]{:S(2)}) copy-start(f32[64]{0:T(128)} %param.21) | copy-start | bytes 772
  23.5 0.7 %copy-start.9 = (f32[12,32]{1,0:T(8,128)S(1)}, f32[12,32]{1,0:T(8,128)}, u32[]{:S(2)}) copy-start(f32[12,32]{1,0:T(8,128)} %param.24) | copy-start | bytes 4612

commit v2 on v1

v2 whole, which is shorter than its diff:
```python
import functools
import math

import jax
import jax.numpy as jnp
from jax import lax
from jax.experimental import pallas as pl
from jax.experimental.pallas import tpu as pltpu
from jax.sharding import PartitionSpec as P

STEPS = 28
MESH = pl.DeviceIdType.MESH

epsilon = 1e-06
guidance = 3.5
shift_factor = 3.0
masked_score = -1e30

SLOT_ROWS = 16
PACK = 4


def sigma_at(position):
    time_left = 1.0 - position / STEPS
    return shift_factor * time_left / (1.0 + (shift_factor - 1.0) * time_left)


def exchange_kernel(
    plan,
    q_hbm, k_hbm, v_hbm, tk_hbm, tv_hbm, gq_hbm, gk_hbm, gt_hbm, len_ref, blk_ref, lat_hbm, base_hbm, w_hbm, step_ref,
    next_ref, clean_ref,
    q_in, k_in, v_in, tk_in, tv_in, gq_ref, gk_ref, gt_ref, lat_in, base_in, w_in,
    stage, recv, packed, wide, parts, recv2,
    load_sem, send_sem, recv_sem, send2_sem, recv2_sem,
):
    n, group, heads, head_size, rows, texts, half = plan
    row_groups = rows // PACK
    units = (heads - group) * row_groups
    unit_start = (group - units) // 2
    blocks = n // group
    f32, bf16 = jnp.float32, jnp.bfloat16
    cfg = lax.axis_index("cfg")
    me = lax.axis_index("seq")
    place = lax.rem(me, group)
    first = me - place
    unit = place - unit_start
    has_unit = (unit >= 0) & (unit < units)
    unit = jnp.clip(unit, 0, units - 1)
    unit_head = group + lax.div(unit, row_groups)
    unit_part = lax.rem(unit, row_groups)

    def each(start, stop, body):
        if stop - start <= 32:
            for i in range(start, stop):
                body(i)
        else:
            def step(i, carry):
                body(i)
                return carry
            lax.fori_loop(start, stop, step, 0)

    def wrapped(value, size):
        return jnp.where(value >= size, value - size, value)

    loads = []
    sources = (
        (k_hbm.at[0], k_in), (tk_hbm.at[0], tk_in), (q_hbm.at[0], q_in), (v_hbm.at[0], v_in), (tv_hbm.at[0], tv_in),
        (gq_hbm, gq_ref), (gk_hbm, gk_ref), (gt_hbm, gt_ref),
        (lat_hbm, lat_in), (base_hbm.at[0], base_in), (w_hbm, w_in),
    )
    for i, (src, dst) in enumerate(sources):
        load = pltpu.make_async_copy(src, dst, load_sem.at[i])
        load.start()
        loads.append(load)

    barrier = pltpu.get_barrier_semaphore()

    def greet_half(i):
        pl.semaphore_signal(barrier, inc=1, device_id=(cfg, wrapped(me + i, n)), device_id_type=MESH)

    def greet_other(i):
        pl.semaphore_signal(barrier, inc=1, device_id=(1 - cfg, first + i), device_id_type=MESH)

    each(1, n, greet_half)
    each(0, group, greet_other)

    lane = lax.broadcasted_iota(jnp.int32, (SLOT_ROWS, 128), 1)
    row = lax.broadcasted_iota(jnp.int32, (SLOT_ROWS, 128), 0)
    low = lane < head_size
    is_text = (row >= rows) & (row < rows + texts)
    slot_index = me * texts + row - rows
    open_row = (row < rows) | (is_text & (slot_index < len_ref[0]) & (blk_ref[0, 0] == 1))
    bias = jnp.where((lane == 0) & jnp.logical_not(open_row), masked_score, 0.0)

    def chunk(ref, c):
        part = ref[:, c * 128:min((c + 1) * 128, heads * head_size)].astype(f32)
        if part.shape[1] < 128:
            part = jnp.concatenate([part, jnp.zeros((part.shape[0], 128 - part.shape[1]), f32)], axis=1)
        return part

    def tall(part):
        return jnp.concatenate([part, jnp.zeros((SLOT_ROWS - part.shape[0], 128), f32)], axis=0)

    def with_text(part, text):
        if texts == 1:
            return jnp.where(row == rows, text, tall(part))
        return tall(jnp.concatenate([part, text], axis=0))

    def normed(part, gain):
        square = part * part
        left = jnp.sum(jnp.where(low, square, 0.0), axis=1, keepdims=True)
        right = jnp.sum(jnp.where(low, 0.0, square), axis=1, keepdims=True)
        mean = jnp.where(low, left, right) * (1.0 / head_size)
        return part * lax.rsqrt(mean + epsilon) * gain

    for load in loads[:8]:
        load.wait()
    gain_q = jnp.concatenate([gq_ref[...], gq_ref[...]], axis=1) * (1.0 / math.sqrt(head_size))
    gain_k = jnp.concatenate([gk_ref[...], gk_ref[...]], axis=1)
    gain_t = jnp.concatenate([gt_ref[...], gt_ref[...]], axis=1)
    gain_kt = jnp.where(is_text, gain_t, gain_k)
    for c in range((heads + 1) // 2):
        qn = normed(tall(chunk(q_in, c)), gain_q)
        kn = normed(with_text(chunk(k_in, c), chunk(tk_in, c)), gain_kt)
        vv = with_text(chunk(v_in, c), chunk(tv_in, c))
        q_turn = pltpu.roll(qn, head_size, 1)
        k_turn = pltpu.roll(kn, head_size, 1)
        v_turn = pltpu.roll(vv, head_size, 1)
        stage[2 * c, :, 0:128] = jnp.where(low, bias, k_turn).astype(bf16)
        stage[2 * c, :, 128:256] = jnp.where(low, vv, q_turn).astype(bf16)
        if 2 * c + 1 < heads:
            stage[2 * c + 1, :, 0:128] = jnp.where(low, bias, kn).astype(bf16)
            stage[2 * c + 1, :, 128:256] = jnp.where(low, v_turn, qn).astype(bf16)

    pl.semaphore_wait(barrier, n - 1 + group)

    def send_head(peer, slot, head):
        pltpu.make_async_remote_copy(
            src_ref=stage.at[head],
            dst_ref=recv.at[slot, me],
            send_sem=send_sem.at[slot],
            recv_sem=recv_sem.at[slot],
            device_id=(cfg, peer),
            device_id_type=MESH,
        ).start()

    def send_unit(block):
        for u in range(units):
            peer = block * group + unit_start + u

            @pl.when(peer != me)
            def _():
                send_head(peer, 1, group + u // row_groups)

    def send_own(i):
        peer = wrapped(me + i, n)
        send_head(peer, 0, lax.rem(peer, group) if n > group else peer)

    each(0, blocks, send_unit)
    each(1, n, send_own)
    recv[0, me] = stage[place]

    @pl.when(has_unit)
    def _():
        recv[1, me] = stage[unit_head]

    @pl.when(jnp.logical_not(has_unit))
    def _():
        recv[1] = jnp.zeros(recv.shape[1:], bf16)

    for load in loads[8:]:
        load.wait()
    wide[...] = jnp.zeros(wide.shape, bf16)
    lane_w = lax.broadcasted_iota(jnp.int32, (2 * half, 128), 1)
    full = (heads * head_size) // 128
    for slot, head in ((0, place), (1, unit_head)):
        pair = lax.div(head, 2)
        start = pl.multiple_of(jnp.minimum(pair, full - 1) * 128, 128)
        weight = w_in[:, pl.ds(start, 128)].astype(f32)
        if full * 128 < heads * head_size:
            weight = jnp.where(pair == full, chunk(w_in, full), weight)
        weight = jnp.where(lax.rem(head, 2) == 1, pltpu.roll(weight, head_size, 1), weight)
        weight = jnp.where(lane_w < head_size, weight, 0.0).astype(bf16)
        for side in range(2):
            for g in range(row_groups):
                at = side * 128 + g * half
                wide[slot, g, at:at + half, :] = weight[side * half:(side + 1) * half]
    base = base_in[...].astype(f32)
    base_packed = []
    for side in range(2):
        pieces = [base[g * PACK:(g + 1) * PACK, side * half:(side + 1) * half] for g in range(row_groups)]
        pieces.append(jnp.zeros((PACK, 128 - row_groups * half), f32))
        base_packed.append(jnp.concatenate(pieces, axis=1))
    step_now = jnp.full((PACK, half), step_ref[0], jnp.int32).astype(f32)
    sigma_now = sigma_at(step_now)
    sigma_gain = sigma_at(step_now + 1.0) - sigma_now

    def whole_wait(buffer, count, sem):
        span = buffer.at[pl.ds(0, count)]
        pltpu.make_async_copy(span, span, sem).wait()

    whole_wait(recv.at[0], n - 1, recv_sem.at[0])

    @pl.when(has_unit)
    def _():
        whole_wait(recv.at[1], n - 1, recv_sem.at[1])

    for s in range(group):
        own = recv[0, first + s, :, 128:256].astype(f32)
        for g in range(row_groups):
            packed[g, s * PACK:(s + 1) * PACK, :] = own[g * PACK:(g + 1) * PACK]
        own = recv[1, first + s, :, 128:256].astype(f32)
        chosen = own[0:PACK]
        for g in range(1, row_groups):
            chosen = jnp.where(unit_part == g, own[g * PACK:(g + 1) * PACK], chosen)
        packed[row_groups, s * PACK:(s + 1) * PACK, :] = chosen

    lane_q = lax.broadcasted_iota(jnp.int32, (group * PACK, 128), 1)
    nt = (((1,), (1,)), ((), ()))
    total = None
    for c in range(row_groups + 1):
        slot, part = (0, c) if c < row_groups else (1, unit_part)
        keys = recv[slot, :, :, 0:128].reshape(n * SLOT_ROWS, 128)
        values = recv[slot, :, :, 128:256].reshape(n * SLOT_ROWS, 128)
        query = jnp.where(lane_q < head_size, jnp.where(lane_q == 0, 1.0, 0.0), packed[c]).astype(bf16)
        scores = lax.dot_general(query, keys, nt, preferred_element_type=f32)
        top = jnp.max(scores, axis=1, keepdims=True)
        weights = jnp.exp(scores - top)
        den = jnp.sum(weights, axis=1, keepdims=True)
        num = jnp.dot(weights.astype(bf16), values, preferred_element_type=f32)
        attended = (num / den).astype(bf16)
        term = lax.dot_general(attended, wide[slot, part], nt, preferred_element_type=f32)
        total = term if total is None else total + term
    for side in range(2):
        for s in range(group):
            parts[side, s] = total[s * PACK:(s + 1) * PACK, side * 128:(side + 1) * 128]
    for side in range(2):
        parts[side, place] = parts[side, place] + base_packed[side]

    mine = cfg * group + place

    def send_part(i):
        target = wrapped(mine + i, 2 * group)
        side = jnp.where(target >= group, 1, 0)
        s = target - side * group
        pltpu.make_async_remote_copy(
            src_ref=parts.at[side, s],
            dst_ref=recv2.at[mine],
            send_sem=send2_sem,
            recv_sem=recv2_sem,
            device_id=(side, first + s),
            device_id_type=MESH,
        ).start()

    each(1, 2 * group, send_part)
    recv2[mine] = parts[cfg, place]

    whole_wait(recv.at[0], n - 1, send_sem.at[0])

    @pl.when(has_unit)
    def _():
        whole_wait(recv.at[1], units * blocks - 1, send_sem.at[1])

    @pl.when(jnp.logical_not(has_unit))
    def _():
        whole_wait(recv.at[1], units * blocks, send_sem.at[1])

    whole_wait(recv2, 2 * group - 1, recv2_sem)
    cond = jnp.sum(recv2[0:group], axis=0)
    uncond = jnp.sum(recv2[group:2 * group], axis=0)
    guided = uncond + guidance * (cond - uncond)
    for g in range(row_groups):
        span = slice(g * PACK, (g + 1) * PACK)
        piece = guided[:, g * half:(g + 1) * half]
        latent = lat_in[span, :]
        next_ref[span, :] = latent + sigma_gain * piece
        clean_ref[span, :] = latent - sigma_now * piece

    whole_wait(recv2, 2 * group - 1, send2_sem)


def on_device(
    n,
    img_queries, img_keys, img_values, text_keys, text_values, query_gain, key_gain, text_gain,
    text_lengths, text_blocks, latent, base_velocity, out_weight, timestep,
):
    head_size = query_gain.shape[0]
    width = img_queries.shape[2]
    heads = width // head_size
    rows, texts = img_queries.shape[1], text_keys.shape[1]
    half = latent.shape[1]
    group = max(d for d in range(1, min(n, heads) + 1) if n % d == 0)
    plan = (n, group, heads, head_size, rows, texts, half)
    bf16, f32 = jnp.bfloat16, jnp.float32
    hbm = pl.BlockSpec(memory_space=pltpu.HBM)
    vmem = pl.BlockSpec(memory_space=pltpu.VMEM)
    smem = pl.BlockSpec(memory_space=pltpu.SMEM)
    return pl.pallas_call(
        functools.partial(exchange_kernel, plan),
        out_shape=[jax.ShapeDtypeStruct((rows, half), f32)] * 2,
        in_specs=[hbm] * 8 + [smem] * 2 + [hbm] * 3 + [smem],
        out_specs=[vmem] * 2,
        scratch_shapes=[
            pltpu.VMEM((rows, width), bf16),
            pltpu.VMEM((rows, width), bf16),
            pltpu.VMEM((rows, width), bf16),
            pltpu.VMEM((texts, width), bf16),
            pltpu.VMEM((texts, width), bf16),
            pltpu.VMEM((1, head_size), f32),
            pltpu.VMEM((1, head_size), f32),
            pltpu.VMEM((1, head_size), f32),
            pltpu.VMEM((rows, half), f32),
            pltpu.VMEM((rows, 2 * half), bf16),
            pltpu.VMEM((2 * half, width), bf16),
            pltpu.VMEM((heads, SLOT_ROWS, 256), bf16),
            pltpu.VMEM((2, n, SLOT_ROWS, 256), bf16),
            pltpu.VMEM((rows // PACK + 1, group * PACK, 128), f32),
            pltpu.VMEM((2, rows // PACK, 256, 128), bf16),
            pltpu.VMEM((2, group, PACK, 128), f32),
            pltpu.VMEM((2 * group, PACK, 128), f32),
            pltpu.SemaphoreType.DMA((11,)),
            pltpu.SemaphoreType.DMA((2,)),
            pltpu.SemaphoreType.DMA((2,)),
            pltpu.SemaphoreType.DMA,
            pltpu.SemaphoreType.DMA,
        ],
        compiler_params=pltpu.CompilerParams(
            collective_id=0, has_side_effects=True, vmem_limit_bytes=63 * 1024 * 1024
        ),
    )(
        img_queries, img_keys, img_values, text_keys, text_values,
        query_gain.reshape(1, -1), key_gain.reshape(1, -1), text_gain.reshape(1, -1),
        text_lengths, text_blocks, latent, base_velocity, out_weight.T, timestep,
    )


def solution(mesh):
    return jax.shard_map(
        functools.partial(on_device, mesh.shape["seq"]),
        mesh=mesh,
        in_specs=(
            P("cfg", "seq", None),
            P("cfg", "seq", None),
            P("cfg", "seq", None),
            P("cfg", "seq", None),
            P("cfg", "seq", None),
            P(),
            P(),
            P(),
            P("cfg"),
            P("cfg", "seq"),
            P("seq", "cfg"),
            P("cfg", "seq", None),
            P(),
            P(),
        ),
        out_specs=(P("seq", "cfg"), P("seq", "cfg")),
        check_vma=False,
    )
```

time: 25 us -> 24.8 us (level)
  other arithmetic: 0.61 us -> 0 us
  Pallas kernels: 19.5 us -> 20.1 us
    pallas_call x1, Pallas kernels: 19.5 us -> 20.1 us  [on_device(): pl.pallas_call(functools.partial(exchange_kernel, plan), out_shape=[jax.S...]
    sub x1 -> x0, other arithmetic: 0.61 us -> none  [on_device(): denoised = latent - sigma_now * guided]
    unnamed x21 -> x4, local copies, waits for them, and re-layouts: 1.88 us -> 1.9 us
where the time goes in v2:
time: 24.8 us; the launch traced here: 24.6 us
  Pallas kernels  20.1 us (81%)
  between operations  2.59 us (10%)
  local copies, waits for them, and re-layouts  1.9 us (8%)
    pallas_call x1, Pallas kernels, on_device(): pl.pallas_call(functools.partial(exchange_kernel, plan), out_shape=[jax.S...  20.1 us
    unnamed x4, local copies, waits for them, and re-layouts  1.9 us

profile of v2, /device:TPU:0, one launch (start us, length us, event | category | flops | bytes accessed | tf_op | source)
XLA Modules:
  0.0 24.6 jit_solution(418945826715518112)
XLA Ops:
  2.6 20.1 %shard_map.149 = (f32[12,32]{1,0:T(8,128)}, f32[12,32]{1,0:T(8,128)}) custom-call(bf16[1,12,1216]{2,1,0:T(8,128)(2,1)} %q_hbm.1, bf16[1,12,1216]{2,1,0:T(8,128)(2,1)} %k_hbm.1, bf16[1,12,1216]{2,1,0:T(8,128)(2,1)} %v_hbm.1, bf16[1,1,1216]{2,1,0:T(2,128)(2,1)} %tk_hbm.1, bf16[1,1,1216]{2,1,0:T(2,128)(2,1)} %tv_hbm.1, f32[1,64]{1,0:T(1,128)} %bitcast.5, ...), custom_call_target="tpu_custom_call" | custom-call | tf_op jit(solution)/shard_map/pallas_call | solution.py:298
  22.7 0.0 copy-start
  22.7 1.3 %copy.21 = f32[12,32]{1,0:T(8,128)} copy(f32[12,32]{1,0:T(8,128)} %get-tuple-element.4) | data formatting | bytes 3072
  24.0 0.0 copy-done
  24.0 0.6 %copy.22 = f32[12,32]{1,0:T(8,128)} copy(f32[12,32]{1,0:T(8,128)S(1)} %copy-done) | data formatting | bytes 3072
Async XLA Ops:
  22.7 1.3 %copy-start = (f32[12,32]{1,0:T(8,128)S(1)}, f32[12,32]{1,0:T(8,128)}, u32[]{:S(2)}) copy-start(f32[12,32]{1,0:T(8,128)} %get-tuple-element.5) | copy-start | bytes 4612

commit v3 on v2

v3 whole, which is shorter than its diff:
```python
import functools
import math

import jax
import jax.numpy as jnp
from jax import lax
from jax.experimental import pallas as pl
from jax.experimental.pallas import tpu as pltpu
from jax.sharding import PartitionSpec as P

STEPS = 28
MESH = pl.DeviceIdType.MESH

epsilon = 1e-06
guidance = 3.5
shift_factor = 3.0
masked_score = -1e30

SLOT_ROWS = 16
PACK = 4


def sigma_at(position):
    time_left = 1.0 - position / STEPS
    return shift_factor * time_left / (1.0 + (shift_factor - 1.0) * time_left)


def exchange_kernel(
    plan,
    q_hbm, k_hbm, v_hbm, tk_hbm, tv_hbm, gq_hbm, gk_hbm, gt_hbm, len_ref, blk_ref, lat_hbm, base_hbm, w_hbm, step_ref,
    out_ref,
    q_in, k_in, v_in, tk_in, tv_in, gq_ref, gk_ref, gt_ref, lat_in, base_in, w_in,
    stage, recv, packed, parts, recv2,
    load_sem, send_sem, recv_sem, send2_sem, recv2_sem,
):
    n, team, heads, head_size, rows, texts, half = plan
    row_groups = rows // PACK
    own_heads = heads // team
    extras = heads - own_heads * team
    slots = own_heads + (1 if extras else 0)
    stride = max(1, team // max(1, extras))
    if stride * (extras - 1) + 1 > team:
        stride = 1
    teams = n // team
    tile = SLOT_ROWS
    f32, bf16 = jnp.float32, jnp.bfloat16
    cfg = lax.axis_index("cfg")
    me = lax.axis_index("seq")
    place = lax.rem(me, team)
    first = me - place
    extra = jnp.minimum(lax.div(place, stride), max(extras - 1, 0))
    has_extra = (lax.rem(place, stride) == 0) & (lax.div(place, stride) < extras)
    extra_head = own_heads * team + extra

    def wrapped(value, size):
        return jnp.where(value >= size, value - size, value)

    def each_team(body):
        if teams <= 4:
            for t in range(1, teams):
                body(t)
        else:
            def step(t, carry):
                body(t)
                return carry
            lax.fori_loop(1, teams, step, 0)

    loads = []
    sources = (
        (k_hbm.at[0], k_in), (tk_hbm.at[0], tk_in), (q_hbm.at[0], q_in), (v_hbm.at[0], v_in), (tv_hbm.at[0], tv_in),
        (gq_hbm, gq_ref), (gk_hbm, gk_ref), (gt_hbm, gt_ref),
        (lat_hbm, lat_in), (base_hbm.at[0], base_in), (w_hbm, w_in),
    )
    for i, (src, dst) in enumerate(sources):
        load = pltpu.make_async_copy(src, dst, load_sem.at[i])
        load.start()
        loads.append(load)

    barrier = pltpu.get_barrier_semaphore()

    def greet(side, peer):
        pl.semaphore_signal(barrier, inc=1, device_id=(side, peer), device_id_type=MESH)

    def greet_team(t):
        other = wrapped(first + t * team, n)
        for i in range(team):
            greet(cfg, other + i)

    each_team(greet_team)
    for i in range(1, team):
        greet(cfg, first + wrapped(place + i, team))
    for i in range(team):
        greet(1 - cfg, first + i)

    lane = lax.broadcasted_iota(jnp.int32, (tile, 128), 1)
    row = lax.broadcasted_iota(jnp.int32, (tile, 128), 0)
    low = lane < head_size
    is_text = (row >= rows) & (row < rows + texts)
    is_flag = (lane == 0) & (row >= rows + texts) & (row < rows + 2 * texts)
    slot_index = me * texts + row - rows - texts
    flags = jnp.where(is_flag & (slot_index < len_ref[0]) & (blk_ref[0, 0] == 1), 1.0, 0.0)

    def chunk(ref, c):
        part = ref[:, c * 128:min((c + 1) * 128, heads * head_size)].astype(f32)
        if part.shape[1] < 128:
            part = jnp.concatenate([part, jnp.zeros((part.shape[0], 128 - part.shape[1]), f32)], axis=1)
        return part

    def tall(part):
        return jnp.concatenate([part, jnp.zeros((tile - part.shape[0], 128), f32)], axis=0)

    def with_text(part, text):
        if texts == 1:
            return jnp.where(row == rows, text, tall(part))
        return tall(jnp.concatenate([part, text], axis=0))

    def normed(part, gain):
        square = part * part
        left = jnp.sum(jnp.where(low, square, 0.0), axis=1, keepdims=True)
        right = jnp.sum(jnp.where(low, 0.0, square), axis=1, keepdims=True)
        mean = jnp.where(low, left, right) * (1.0 / head_size)
        return part * lax.rsqrt(mean + epsilon) * gain

    for load in loads[:8]:
        load.wait()
    gain_q = jnp.concatenate([gq_ref[...], gq_ref[...]], axis=1) * (1.0 / math.sqrt(head_size))
    gain_k = jnp.concatenate([gk_ref[...], gk_ref[...]], axis=1)
    gain_t = jnp.concatenate([gt_ref[...], gt_ref[...]], axis=1)
    gain_kt = jnp.where(is_text, gain_t, gain_k)
    for c in range((heads + 1) // 2):
        qn = normed(tall(chunk(q_in, c)), gain_q)
        kn = normed(with_text(chunk(k_in, c), chunk(tk_in, c)), gain_kt)
        vv = with_text(chunk(v_in, c), chunk(tv_in, c))
        q_turn = pltpu.roll(qn, head_size, 1)
        k_turn = pltpu.roll(kn, head_size, 1)
        v_turn = pltpu.roll(vv, head_size, 1)
        stage[2 * c, 0:tile] = (jnp.where(low, kn, v_turn) + flags).astype(bf16)
        stage[2 * c, tile:2 * tile] = jnp.where(low, qn, 0.0).astype(bf16)
        if 2 * c + 1 < heads:
            stage[2 * c + 1, 0:tile] = (jnp.where(low, k_turn, vv) + flags).astype(bf16)
            stage[2 * c + 1, tile:2 * tile] = jnp.where(low, q_turn, 0.0).astype(bf16)

    pl.semaphore_wait(barrier, n - 1 + team)

    def send(src, dst, kind, peer):
        pltpu.make_async_remote_copy(
            src_ref=src,
            dst_ref=dst,
            send_sem=send_sem.at[kind],
            recv_sem=recv_sem.at[kind],
            device_id=(cfg, peer),
            device_id_type=MESH,
        ).start()

    def send_team(t):
        other = wrapped(first + t * team, n)
        for e in range(extras):
            send(
                stage.at[own_heads * team + e, pl.ds(0, tile)], recv.at[me, own_heads, pl.ds(0, tile)],
                2, other + e * stride,
            )
        for i in range(team):
            p = wrapped(place + i, team)
            send(
                stage.at[pl.ds(p * own_heads, own_heads), pl.ds(0, tile)],
                recv.at[me, pl.ds(0, own_heads), pl.ds(0, tile)],
                0, other + p,
            )

    each_team(send_team)
    for e in range(extras):
        @pl.when(place != e * stride)
        def _():
            send(stage.at[own_heads * team + e], recv.at[me, own_heads], 3, first + e * stride)

    for i in range(1, team):
        p = wrapped(place + i, team)
        send(stage.at[pl.ds(p * own_heads, own_heads)], recv.at[me, pl.ds(0, own_heads)], 1, first + p)

    for j in range(own_heads):
        recv[me, j] = stage[place * own_heads + j]
    if extras:
        @pl.when(has_extra)
        def _():
            recv[me, own_heads] = stage[extra_head]

        @pl.when(jnp.logical_not(has_extra))
        def _():
            recv[:, own_heads] = jnp.zeros((n, 2 * tile, 128), bf16)

    for load in loads[8:]:
        load.wait()
    lane_w = lax.broadcasted_iota(jnp.int32, (2 * half, 128), 1)
    full = (heads * head_size) // 128
    head_weights = []
    for j in range(slots):
        head = place * own_heads + j if j < own_heads else extra_head
        pair = lax.div(head, 2)
        start = pl.multiple_of(jnp.minimum(pair, full - 1) * 128, 128)
        weight = w_in[:, pl.ds(start, 128)].astype(f32)
        if full * 128 < heads * head_size:
            weight = jnp.where(pair == full, chunk(w_in, full), weight)
        weight = jnp.where(lax.rem(head, 2) == 0, pltpu.roll(weight, head_size, 1), weight)
        head_weights.append(jnp.where(lane_w < head_size, 0.0, weight).astype(bf16))
    base = base_in[...].astype(f32)
    base_packed = []
    for side in range(2):
        pieces = [base[g * PACK:(g + 1) * PACK, side * half:(side + 1) * half] for g in range(row_groups)]
        pieces.append(jnp.zeros((PACK, 128 - row_groups * half), f32))
        base_packed.append(jnp.concatenate(pieces, axis=1))
    step_now = jnp.full((PACK, half), step_ref[0], jnp.int32).astype(f32)
    sigma_now = sigma_at(step_now)
    sigma_gain = sigma_at(step_now + 1.0) - sigma_now

    def whole_wait(span, sem):
        pltpu.make_async_copy(span, span, sem).wait()

    far = pl.ds(0, n - team)
    near = pl.ds(0, team - 1)
    whole_wait(recv.at[near, pl.ds(0, own_heads)], recv_sem.at[1])
    whole_wait(recv.at[far, pl.ds(0, own_heads), pl.ds(0, tile)], recv_sem.at[0])
    if extras:
        @pl.when(has_extra)
        def _():
            whole_wait(recv.at[near, own_heads], recv_sem.at[3])
            whole_wait(recv.at[far, own_heads, pl.ds(0, tile)], recv_sem.at[2])

    for s in range(team):
        for j in range(slots):
            own = recv[first + s, j, tile:2 * tile].astype(f32)
            for g in range(row_groups):
                at = (g * team + s) * PACK
                packed[j, at:at + PACK, :] = own[g * PACK:(g + 1) * PACK]

    nt = (((1,), (1,)), ((), ()))
    picker = jnp.where(lax.broadcasted_iota(jnp.int32, (8, 128), 1) == 0, 1.0, 0.0).astype(bf16)
    total = None
    bias = None
    for j in range(slots):
        pairs = recv[:, j, 0:tile].reshape(n * tile, 128)
        if bias is None:
            seen = lax.dot_general(picker, pairs, nt, preferred_element_type=f32)
            seen = pltpu.roll(seen, n * tile - texts, 1)[0:1]
            key_row = lax.rem(lax.broadcasted_iota(jnp.int32, (1, n * tile), 1), tile)
            open_key = (key_row < rows) | ((key_row < rows + texts) & (seen > 0.5))
            bias = jnp.where(open_key, 0.0, masked_score)
        scores = lax.dot_general(packed[j].astype(bf16), pairs, nt, preferred_element_type=f32) + bias
        top = jnp.max(scores, axis=1, keepdims=True)
        weights = jnp.exp(scores - top)
        den = jnp.sum(weights, axis=1, keepdims=True)
        num = jnp.dot(weights.astype(bf16), pairs, preferred_element_type=f32)
        attended = (num / den).astype(bf16)
        term = lax.dot_general(attended, head_weights[j], nt, preferred_element_type=f32)
        total = term if total is None else total + term

    span = team * PACK
    for side in range(2):
        pieces = [total[g * span:(g + 1) * span, side * half:(side + 1) * half] for g in range(row_groups)]
        pieces.append(jnp.zeros((span, 128 - row_groups * half), f32))
        block = jnp.concatenate(pieces, axis=1)
        for s in range(team):
            parts[side, s] = block[s * PACK:(s + 1) * PACK]
    for side in range(2):
        parts[side, place] = parts[side, place] + base_packed[side]

    mine = cfg * team + place

    def send_part(side, s):
        pltpu.make_async_remote_copy(
            src_ref=parts.at[side, s],
            dst_ref=recv2.at[mine],
            send_sem=send2_sem,
            recv_sem=recv2_sem,
            device_id=(side, first + s),
            device_id_type=MESH,
        ).start()

    for i in range(team):
        send_part(1 - cfg, wrapped(place + i, team))
    for i in range(1, team):
        send_part(cfg, wrapped(place + i, team))
    recv2[mine] = parts[cfg, place]

    whole_wait(recv.at[near, pl.ds(0, own_heads)], send_sem.at[1])
    whole_wait(recv.at[far, pl.ds(0, own_heads), pl.ds(0, tile)], send_sem.at[0])
    if extras:
        whole_wait(recv.at[pl.ds(0, extras * (teams - 1)), own_heads, pl.ds(0, tile)], send_sem.at[2])

        @pl.when(jnp.logical_not(has_extra))
        def _():
            whole_wait(recv.at[pl.ds(0, extras), own_heads], send_sem.at[3])
        if extras > 1:
            @pl.when(has_extra)
            def _():
                whole_wait(recv.at[pl.ds(0, extras - 1), own_heads], send_sem.at[3])

    whole_wait(recv2.at[pl.ds(0, 2 * team - 1)], recv2_sem)
    cond = jnp.sum(recv2[0:team], axis=0)
    uncond = jnp.sum(recv2[team:2 * team], axis=0)
    guided = uncond + guidance * (cond - uncond)
    for g in range(row_groups):
        at = slice(g * PACK, (g + 1) * PACK)
        piece = guided[:, g * half:(g + 1) * half]
        latent = lat_in[at, :]
        out_ref[0, at, :] = latent + sigma_gain * piece
        out_ref[1, at, :] = latent - sigma_now * piece

    whole_wait(recv2.at[pl.ds(0, 2 * team - 1)], send2_sem)


def on_device(
    n,
    img_queries, img_keys, img_values, text_keys, text_values, query_gain, key_gain, text_gain,
    text_lengths, text_blocks, latent, base_velocity, out_weight, timestep,
):
    head_size = query_gain.shape[0]
    width = img_queries.shape[2]
    heads = width // head_size
    rows, texts = img_queries.shape[1], text_keys.shape[1]
    half = latent.shape[1]
    team = max(d for d in range(1, min(n // 2, heads, 8) + 1) if n % d == 0)
    slots = -(-heads // team)
    plan = (n, team, heads, head_size, rows, texts, half)
    bf16, f32 = jnp.bfloat16, jnp.float32
    hbm = pl.BlockSpec(memory_space=pltpu.HBM)
    vmem = pl.BlockSpec(memory_space=pltpu.VMEM)
    smem = pl.BlockSpec(memory_space=pltpu.SMEM)
    both = pl.pallas_call(
        functools.partial(exchange_kernel, plan),
        out_shape=jax.ShapeDtypeStruct((2, rows, half), f32),
        in_specs=[hbm] * 8 + [smem] * 2 + [hbm] * 3 + [smem],
        out_specs=vmem,
        scratch_shapes=[
            pltpu.VMEM((rows, width), bf16),
            pltpu.VMEM((rows, width), bf16),
            pltpu.VMEM((rows, width), bf16),
            pltpu.VMEM((texts, width), bf16),
            pltpu.VMEM((texts, width), bf16),
            pltpu.VMEM((1, head_size), f32),
            pltpu.VMEM((1, head_size), f32),
            pltpu.VMEM((1, head_size), f32),
            pltpu.VMEM((rows, half), f32),
            pltpu.VMEM((rows, 2 * half), bf16),
            pltpu.VMEM((2 * half, width), bf16),
            pltpu.VMEM((heads, 2 * SLOT_ROWS, 128), bf16),
            pltpu.VMEM((n, slots, 2 * SLOT_ROWS, 128), bf16),
            pltpu.VMEM((slots, team * rows, 128), f32),
            pltpu.VMEM((2, team, PACK, 128), f32),
            pltpu.VMEM((2 * team, PACK, 128), f32),
            pltpu.SemaphoreType.DMA((11,)),
            pltpu.SemaphoreType.DMA((4,)),
            pltpu.SemaphoreType.DMA((4,)),
            pltpu.SemaphoreType.DMA,
            pltpu.SemaphoreType.DMA,
        ],
        compiler_params=pltpu.CompilerParams(
            collective_id=0, has_side_effects=True, vmem_limit_bytes=63 * 1024 * 1024
        ),
    )(
        img_queries, img_keys, img_values, text_keys, text_values,
        query_gain.reshape(1, -1), key_gain.reshape(1, -1), text_gain.reshape(1, -1),
        text_lengths, text_blocks, latent, base_velocity, out_weight.T, timestep,
    )
    return (both[0], both[1])


def solution(mesh):
    return jax.shard_map(
        functools.partial(on_device, mesh.shape["seq"]),
        mesh=mesh,
        in_specs=(
            P("cfg", "seq", None),
            P("cfg", "seq", None),
            P("cfg", "seq", None),
            P("cfg", "seq", None),
            P("cfg", "seq", None),
            P(),
            P(),
            P(),
            P("cfg"),
            P("cfg", "seq"),
            P("seq", "cfg"),
            P("cfg", "seq", None),
            P(),
            P(),
        ),
        out_specs=(P("seq", "cfg"), P("seq", "cfg")),
        check_vma=False,
    )
```

time: 24.8 us -> 21.5 us (0.87)
  Pallas kernels: 20.1 us -> 17.4 us
  local copies, waits for them, and re-layouts: 1.9 us -> 1.32 us
    pallas_call x1, Pallas kernels: 20.1 us -> 17.4 us  [on_device(): pl.pallas_call(functools.partial(exchange_kernel, plan), out_shape=jax.Sh...]
    unnamed x4 -> x0, local copies, waits for them, and re-layouts: 1.9 us -> none
    squeeze x0 -> x1, local copies, waits for them, and re-layouts: none -> 1.32 us  [on_device(): return (both[0], both[1])]
where the time goes in v3:
time: 21.5 us; the launch traced here: 21.3 us
  Pallas kernels  17.4 us (81%)
  between operations  2.58 us (12%)
  local copies, waits for them, and re-layouts  1.32 us (6%)
    pallas_call x1, Pallas kernels, on_device(): pl.pallas_call(functools.partial(exchange_kernel, plan), out_shape=jax.Sh...  17.4 us
    squeeze x1, local copies, waits for them, and re-layouts, on_device(): return (both[0], both[1])  1.32 us

profile of v3, /device:TPU:0, one launch (start us, length us, event | category | flops | bytes accessed | tf_op | source)
XLA Modules:
  0.0 21.3 jit_solution(16855435701173159258)
XLA Ops:
  2.6 17.4 %shard_map.149 = f32[2,12,32]{2,1,0:T(8,128)} custom-call(bf16[1,12,1216]{2,1,0:T(8,128)(2,1)} %q_hbm.1, bf16[1,12,1216]{2,1,0:T(8,128)(2,1)} %k_hbm.1, bf16[1,12,1216]{2,1,0:T(8,128)(2,1)} %v_hbm.1, bf16[1,1,1216]{2,1,0:T(2,128)(2,1)} %tk_hbm.1, bf16[1,1,1216]{2,1,0:T(2,128)(2,1)} %tv_hbm.1, f32[1,64]{1,0:T(1,128)} %bitcast.9, f32[1,64]{1,0:T(1,128)} %bitcast.10, ...), custom_call_target="tpu_custom_call" | custom-call | tf_op jit(solution)/shard_map/pallas_call | solution.py:328
  20.0 1.3 %slice_bitcast_fusion = (f32[12,32]{1,0:T(8,128)}, f32[12,32]{1,0:T(8,128)}) fusion(f32[2,12,32]{2,1,0:T(8,128)} %shard_map.149), kind=kLoop, calls=%fused_computation | loop fusion | bytes 6144 | tf_op jit(solution)/shard_map/squeeze | solution.py:364

commit v4 on v3

--- a/solution.py
+++ b/solution.py
@@ -65,6 +65,22 @@
                 return carry
             lax.fori_loop(1, teams, step, 0)
 
+    barrier = pltpu.get_barrier_semaphore()
+
+    def greet(side, peer):
+        pl.semaphore_signal(barrier, inc=1, device_id=(side, peer), device_id_type=MESH)
+
+    def greet_team(t):
+        other = wrapped(first + t * team, n)
+        for i in range(team):
+            greet(cfg, other + i)
+
+    each_team(greet_team)
+    for i in range(1, team):
+        greet(cfg, first + wrapped(place + i, team))
+    for i in range(team):
+        greet(1 - cfg, first + i)
+
     loads = []
     sources = (
         (k_hbm.at[0], k_in), (tk_hbm.at[0], tk_in), (q_hbm.at[0], q_in), (v_hbm.at[0], v_in), (tv_hbm.at[0], tv_in),
@@ -75,22 +91,6 @@
         load = pltpu.make_async_copy(src, dst, load_sem.at[i])
         load.start()
         loads.append(load)
-
-    barrier = pltpu.get_barrier_semaphore()
-
-    def greet(side, peer):
-        pl.semaphore_signal(barrier, inc=1, device_id=(side, peer), device_id_type=MESH)
-
-    def greet_team(t):
-        other = wrapped(first + t * team, n)
-        for i in range(team):
-            greet(cfg, other + i)
-
-    each_team(greet_team)
-    for i in range(1, team):
-        greet(cfg, first + wrapped(place + i, team))
-    for i in range(team):
-        greet(1 - cfg, first + i)
 
     lane = lax.broadcasted_iota(jnp.int32, (tile, 128), 1)
     row = lax.broadcasted_iota(jnp.int32, (tile, 128), 0)
@@ -218,12 +218,10 @@
     far = pl.ds(0, n - team)
     near = pl.ds(0, team - 1)
     whole_wait(recv.at[near, pl.ds(0, own_heads)], recv_sem.at[1])
-    whole_wait(recv.at[far, pl.ds(0, own_heads), pl.ds(0, tile)], recv_sem.at[0])
     if extras:
         @pl.when(has_extra)
         def _():
             whole_wait(recv.at[near, own_heads], recv_sem.at[3])
-            whole_wait(recv.at[far, own_heads, pl.ds(0, tile)], recv_sem.at[2])
 
     for s in range(team):
         for j in range(slots):
@@ -234,21 +232,40 @@
 
     nt = (((1,), (1,)), ((), ()))
     picker = jnp.where(lax.broadcasted_iota(jnp.int32, (8, 128), 1) == 0, 1.0, 0.0).astype(bf16)
+    key_row = lax.rem(lax.broadcasted_iota(jnp.int32, (1, team * tile), 1), tile)
+
+    def pairs_of(j, t):
+        return recv[pl.ds(wrapped(first + t * team, n), team), j, 0:tile].reshape(team * tile, 128)
+
+    def bias_of(t):
+        seen = lax.dot_general(picker, pairs_of(0, t), nt, preferred_element_type=f32)
+        seen = pltpu.roll(seen, team * tile - texts, 1)[0:1]
+        open_key = (key_row < rows) | ((key_row < rows + texts) & (seen > 0.5))
+        return jnp.where(open_key, 0.0, masked_score)
+
+    queries = [packed[j].astype(bf16) for j in range(slots)]
+    scores = [[] for j in range(slots)]
+    for t in range(teams):
+        if t == 1:
+            whole_wait(recv.at[far, pl.ds(0, own_heads), pl.ds(0, tile)], recv_sem.at[0])
+            if extras:
+                @pl.when(has_extra)
+                def _():
+                    whole_wait(recv.at[far, own_heads, pl.ds(0, tile)], recv_sem.at[2])
+        bias = bias_of(t)
+        for j in range(slots):
+            scores[j].append(lax.dot_general(queries[j], pairs_of(j, t), nt, preferred_element_type=f32) + bias)
+
     total = None
-    bias = None
     for j in range(slots):
-        pairs = recv[:, j, 0:tile].reshape(n * tile, 128)
-        if bias is None:
-            seen = lax.dot_general(picker, pairs, nt, preferred_element_type=f32)
-            seen = pltpu.roll(seen, n * tile - texts, 1)[0:1]
-            key_row = lax.rem(lax.broadcasted_iota(jnp.int32, (1, n * tile), 1), tile)
-            open_key = (key_row < rows) | ((key_row < rows + texts) & (seen > 0.5))
-            bias = jnp.where(open_key, 0.0, masked_score)
-        scores = lax.dot_general(packed[j].astype(bf16), pairs, nt, preferred_element_type=f32) + bias
-        top = jnp.max(scores, axis=1, keepdims=True)
-        weights = jnp.exp(scores - top)
-        den = jnp.sum(weights, axis=1, keepdims=True)
-        num = jnp.dot(weights.astype(bf16), pairs, preferred_element_type=f32)
+        top = functools.reduce(jnp.maximum, scores[j])
+        top = jnp.max(top, axis=1, keepdims=True)
+        weights = [jnp.exp(score - top) for score in scores[j]]
+        den = jnp.sum(functools.reduce(jnp.add, weights), axis=1, keepdims=True)
+        num = None
+        for t in range(teams):
+            term = jnp.dot(weights[t].astype(bf16), pairs_of(j, t), preferred_element_type=f32)
+            num = term if num is None else num + term
         attended = (num / den).astype(bf16)
         term = lax.dot_general(attended, head_weights[j], nt, preferred_element_type=f32)
         total = term if total is None else total + term
@@ -327,7 +344,7 @@
     smem = pl.BlockSpec(memory_space=pltpu.SMEM)
     both = pl.pallas_call(
         functools.partial(exchange_kernel, plan),
-        out_shape=jax.ShapeDtypeStruct((2, rows, half), f32),
+        out_shape=pltpu.VMEM((2, rows, half), f32),
         in_specs=[hbm] * 8 + [smem] * 2 + [hbm] * 3 + [smem],
         out_specs=vmem,
         scratch_shapes=[

time: 21.5 us -> 20.1 us (0.935)
  local copies, waits for them, and re-layouts: 1.32 us -> 0.61 us
  Pallas kernels: 17.4 us -> 16.8 us
    squeeze x1, local copies, waits for them, and re-layouts: 1.32 us -> 0.61 us  [on_device(): return (both[0], both[1])]
    pallas_call x1, Pallas kernels: 17.4 us -> 16.8 us  [on_device(): pl.pallas_call(functools.partial(exchange_kernel, plan), out_shape=pltpu....]
where the time goes in v4:
time: 20.1 us; the launch traced here: 20 us
  Pallas kernels  16.8 us (84%)
  between operations  2.58 us (13%)
  local copies, waits for them, and re-layouts  0.61 us (3%)
    pallas_call x1, Pallas kernels, on_device(): pl.pallas_call(functools.partial(exchange_kernel, plan), out_shape=pltpu....  16.8 us
    squeeze x1, local copies, waits for them, and re-layouts, on_device(): return (both[0], both[1])  0.61 us

profile of v4, /device:TPU:0, one launch (start us, length us, event | category | flops | bytes accessed | tf_op | source)
XLA Modules:
  0.0 20.0 jit_solution(14134083946688394848)
XLA Ops:
  2.6 16.8 %shard_map.149 = f32[2,12,32]{2,1,0:T(8,128)S(1)} custom-call(bf16[1,12,1216]{2,1,0:T(8,128)(2,1)} %q_hbm.1, bf16[1,12,1216]{2,1,0:T(8,128)(2,1)} %k_hbm.1, bf16[1,12,1216]{2,1,0:T(8,128)(2,1)} %v_hbm.1, bf16[1,1,1216]{2,1,0:T(2,128)(2,1)} %tk_hbm.1, bf16[1,1,1216]{2,1,0:T(2,128)(2,1)} %tv_hbm.1, f32[1,64]{1,0:T(1,128)} %bitcast.9, f32[1,64]{1,0:T(1,128)} %bitcast.10, ...), custom_call_target="tpu_custom_call" | custom-call | tf_op jit(solution)/shard_map/pallas_call | solution.py:345
  19.4 0.6 %slice_bitcast_fusion = (f32[12,32]{1,0:T(8,128)}, f32[12,32]{1,0:T(8,128)}) fusion(f32[2,12,32]{2,1,0:T(8,128)S(1)} %shard_map.149), kind=kLoop, calls=%fused_computation | loop fusion | bytes 6144 | tf_op jit(solution)/shard_map/squeeze | solution.py:381

commit v5 on v4

--- a/solution.py
+++ b/solution.py
@@ -27,9 +27,9 @@
 
 def exchange_kernel(
     plan,
-    q_hbm, k_hbm, v_hbm, tk_hbm, tv_hbm, gq_hbm, gk_hbm, gt_hbm, len_ref, blk_ref, lat_hbm, base_hbm, w_hbm, step_ref,
+    q_hbm, k_hbm, v_hbm, tk_hbm, tv_hbm, gq_hbm, gk_hbm, gt_hbm, len_hbm, blk_hbm, lat_hbm, base_hbm, w_hbm, step_hbm,
     out_ref,
-    q_in, k_in, v_in, tk_in, tv_in, gq_ref, gk_ref, gt_ref, lat_in, base_in, w_in,
+    q_in, k_in, v_in, tk_in, tv_in, gq_ref, gk_ref, gt_ref, len_ref, blk_ref, step_ref, lat_in, base_in, w_in,
     stage, recv, packed, parts, recv2,
     load_sem, send_sem, recv_sem, send2_sem, recv2_sem,
 ):
@@ -85,6 +85,7 @@
     sources = (
         (k_hbm.at[0], k_in), (tk_hbm.at[0], tk_in), (q_hbm.at[0], q_in), (v_hbm.at[0], v_in), (tv_hbm.at[0], tv_in),
         (gq_hbm, gq_ref), (gk_hbm, gk_ref), (gt_hbm, gt_ref),
+        (len_hbm, len_ref), (blk_hbm, blk_ref), (step_hbm, step_ref),
         (lat_hbm, lat_in), (base_hbm.at[0], base_in), (w_hbm, w_in),
     )
     for i, (src, dst) in enumerate(sources):
@@ -98,8 +99,6 @@
     is_text = (row >= rows) & (row < rows + texts)
     is_flag = (lane == 0) & (row >= rows + texts) & (row < rows + 2 * texts)
     slot_index = me * texts + row - rows - texts
-    flags = jnp.where(is_flag & (slot_index < len_ref[0]) & (blk_ref[0, 0] == 1), 1.0, 0.0)
-
     def chunk(ref, c):
         part = ref[:, c * 128:min((c + 1) * 128, heads * head_size)].astype(f32)
         if part.shape[1] < 128:
@@ -121,8 +120,10 @@
         mean = jnp.where(low, left, right) * (1.0 / head_size)
         return part * lax.rsqrt(mean + epsilon) * gain
 
-    for load in loads[:8]:
+    for load in loads[:10]:
         load.wait()
+    usable = (slot_index < len_ref[...]) & (blk_ref[...] == 1)
+    flags = jnp.where(is_flag & usable, 1.0, 0.0)
     gain_q = jnp.concatenate([gq_ref[...], gq_ref[...]], axis=1) * (1.0 / math.sqrt(head_size))
     gain_k = jnp.concatenate([gk_ref[...], gk_ref[...]], axis=1)
     gain_t = jnp.concatenate([gt_ref[...], gt_ref[...]], axis=1)
@@ -188,7 +189,7 @@
         def _():
             recv[:, own_heads] = jnp.zeros((n, 2 * tile, 128), bf16)
 
-    for load in loads[8:]:
+    for load in loads[10:]:
         load.wait()
     lane_w = lax.broadcasted_iota(jnp.int32, (2 * half, 128), 1)
     full = (heads * head_size) // 128
@@ -208,7 +209,7 @@
         pieces = [base[g * PACK:(g + 1) * PACK, side * half:(side + 1) * half] for g in range(row_groups)]
         pieces.append(jnp.zeros((PACK, 128 - row_groups * half), f32))
         base_packed.append(jnp.concatenate(pieces, axis=1))
-    step_now = jnp.full((PACK, half), step_ref[0], jnp.int32).astype(f32)
+    step_now = jnp.broadcast_to(step_ref[...], (PACK, half)).astype(f32)
     sigma_now = sigma_at(step_now)
     sigma_gain = sigma_at(step_now + 1.0) - sigma_now
 
@@ -341,11 +342,10 @@
     bf16, f32 = jnp.bfloat16, jnp.float32
     hbm = pl.BlockSpec(memory_space=pltpu.HBM)
     vmem = pl.BlockSpec(memory_space=pltpu.VMEM)
-    smem = pl.BlockSpec(memory_space=pltpu.SMEM)
     both = pl.pallas_call(
         functools.partial(exchange_kernel, plan),
         out_shape=pltpu.VMEM((2, rows, half), f32),
-        in_specs=[hbm] * 8 + [smem] * 2 + [hbm] * 3 + [smem],
+        in_specs=[hbm] * 14,
         out_specs=vmem,
         scratch_shapes=[
             pltpu.VMEM((rows, width), bf16),
@@ -356,6 +356,9 @@
             pltpu.VMEM((1, head_size), f32),
             pltpu.VMEM((1, head_size), f32),
             pltpu.VMEM((1, head_size), f32),
+            pltpu.VMEM((1, 1), jnp.int32),
+            pltpu.VMEM((1, 1), jnp.int32),
+            pltpu.VMEM((1, 1), jnp.int32),
             pltpu.VMEM((rows, half), f32),
             pltpu.VMEM((rows, 2 * half), bf16),
             pltpu.VMEM((2 * half, width), bf16),
@@ -364,7 +367,7 @@
             pltpu.VMEM((slots, team * rows, 128), f32),
             pltpu.VMEM((2, team, PACK, 128), f32),
             pltpu.VMEM((2 * team, PACK, 128), f32),
-            pltpu.SemaphoreType.DMA((11,)),
+            pltpu.SemaphoreType.DMA((14,)),
             pltpu.SemaphoreType.DMA((4,)),
             pltpu.SemaphoreType.DMA((4,)),
             pltpu.SemaphoreType.DMA,
@@ -376,7 +379,7 @@
     )(
         img_queries, img_keys, img_values, text_keys, text_values,
         query_gain.reshape(1, -1), key_gain.reshape(1, -1), text_gain.reshape(1, -1),
-        text_lengths, text_blocks, latent, base_velocity, out_weight.T, timestep,
+        text_lengths.reshape(1, 1), text_blocks, latent, base_velocity, out_weight.T, timestep.reshape(1, 1),
     )
     return (both[0], both[1])
 

time: 20.1 us -> 20.2 us (level)
  no operation moved by 1% of the time
where the time goes in v5:
time: 20.2 us; the launch traced here: 20 us
  Pallas kernels  16.8 us (83%)
  between operations  2.58 us (13%)
  local copies, waits for them, and re-layouts  0.61 us (3%)
    pallas_call x1, Pallas kernels, on_device(): pl.pallas_call(functools.partial(exchange_kernel, plan), out_shape=pltpu....  16.8 us
    squeeze x1, local copies, waits for them, and re-layouts, on_device(): return (both[0], both[1])  0.61 us

profile of v5, /device:TPU:0, one launch (start us, length us, event | category | flops | bytes accessed | tf_op | source)
XLA Modules:
  0.0 20.0 jit_solution(83534054535756346)
XLA Ops:
  2.6 16.8 %shard_map.149 = f32[2,12,32]{2,1,0:T(8,128)S(1)} custom-call(bf16[1,12,1216]{2,1,0:T(8,128)(2,1)} %q_hbm.1, bf16[1,12,1216]{2,1,0:T(8,128)(2,1)} %k_hbm.1, bf16[1,12,1216]{2,1,0:T(8,128)(2,1)} %v_hbm.1, bf16[1,1,1216]{2,1,0:T(2,128)(2,1)} %tk_hbm.1, bf16[1,1,1216]{2,1,0:T(2,128)(2,1)} %tv_hbm.1, f32[1,64]{1,0:T(1,128)} %bitcast.13, f32[1,64]{1,0:T(1,128)} %bitcast.14, ...), custom_call_target="tpu_custom_call" | custom-call | tf_op jit(solution)/shard_map/pallas_call | solution.py:345
  19.4 0.6 %slice_bitcast_fusion = (f32[12,32]{1,0:T(8,128)}, f32[12,32]{1,0:T(8,128)}) fusion(f32[2,12,32]{2,1,0:T(8,128)S(1)} %shard_map.149), kind=kLoop, calls=%fused_computation | loop fusion | bytes 6144 | tf_op jit(solution)/shard_map/squeeze | solution.py:384

commit v6 on v5

--- a/solution.py
+++ b/solution.py
@@ -55,6 +55,12 @@
     def wrapped(value, size):
         return jnp.where(value >= size, value - size, value)
 
+    def rolled(start, stop, body):
+        def step(i, carry):
+            body(i)
+            return carry
+        lax.fori_loop(start, stop, step, 0)
+
     def each_team(body):
         if teams <= 4:
             for t in range(1, teams):
@@ -72,14 +78,11 @@
 
     def greet_team(t):
         other = wrapped(first + t * team, n)
-        for i in range(team):
-            greet(cfg, other + i)
+        rolled(0, team, lambda i: greet(cfg, other + i))
 
     each_team(greet_team)
-    for i in range(1, team):
-        greet(cfg, first + wrapped(place + i, team))
-    for i in range(team):
-        greet(1 - cfg, first + i)
+    rolled(1, team, lambda i: greet(cfg, first + wrapped(place + i, team)))
+    rolled(0, team, lambda i: greet(1 - cfg, first + i))
 
     loads = []
     sources = (
@@ -160,7 +163,8 @@
                 stage.at[own_heads * team + e, pl.ds(0, tile)], recv.at[me, own_heads, pl.ds(0, tile)],
                 2, other + e * stride,
             )
-        for i in range(team):
+
+        def send_far(i):
             p = wrapped(place + i, team)
             send(
                 stage.at[pl.ds(p * own_heads, own_heads), pl.ds(0, tile)],
@@ -168,15 +172,19 @@
                 0, other + p,
             )
 
+        rolled(0, team, send_far)
+
     each_team(send_team)
     for e in range(extras):
         @pl.when(place != e * stride)
         def _():
             send(stage.at[own_heads * team + e], recv.at[me, own_heads], 3, first + e * stride)
 
-    for i in range(1, team):
+    def send_near(i):
         p = wrapped(place + i, team)
         send(stage.at[pl.ds(p * own_heads, own_heads)], recv.at[me, pl.ds(0, own_heads)], 1, first + p)
+
+    rolled(1, team, send_near)
 
     for j in range(own_heads):
         recv[me, j] = stage[place * own_heads + j]
@@ -293,10 +301,8 @@
             device_id_type=MESH,
         ).start()
 
-    for i in range(team):
-        send_part(1 - cfg, wrapped(place + i, team))
-    for i in range(1, team):
-        send_part(cfg, wrapped(place + i, team))
+    rolled(0, team, lambda i: send_part(1 - cfg, wrapped(place + i, team)))
+    rolled(1, team, lambda i: send_part(cfg, wrapped(place + i, team)))
     recv2[mine] = parts[cfg, place]
 
     whole_wait(recv.at[near, pl.ds(0, own_heads)], send_sem.at[1])

time: 20.2 us -> 20.2 us (level)
  no operation moved by 1% of the time
where the time goes in v6:
time: 20.2 us; the launch traced here: 20 us
  Pallas kernels  16.8 us (83%)
  between operations  2.58 us (13%)
  local copies, waits for them, and re-layouts  0.61 us (3%)
    pallas_call x1, Pallas kernels, on_device(): pl.pallas_call(functools.partial(exchange_kernel, plan), out_shape=pltpu....  16.8 us
    squeeze x1, local copies, waits for them, and re-layouts, on_device(): return (both[0], both[1])  0.61 us

profile of v6, /device:TPU:0, one launch (start us, length us, event | category | flops | bytes accessed | tf_op | source)
XLA Modules:
  0.0 20.0 jit_solution(15517677722766350751)
XLA Ops:
  2.6 16.8 %shard_map.149 = f32[2,12,32]{2,1,0:T(8,128)S(1)} custom-call(bf16[1,12,1216]{2,1,0:T(8,128)(2,1)} %q_hbm.1, bf16[1,12,1216]{2,1,0:T(8,128)(2,1)} %k_hbm.1, bf16[1,12,1216]{2,1,0:T(8,128)(2,1)} %v_hbm.1, bf16[1,1,1216]{2,1,0:T(2,128)(2,1)} %tk_hbm.1, bf16[1,1,1216]{2,1,0:T(2,128)(2,1)} %tv_hbm.1, f32[1,64]{1,0:T(1,128)} %bitcast.13, f32[1,64]{1,0:T(1,128)} %bitcast.14, ...), custom_call_target="tpu_custom_call" | custom-call | tf_op jit(solution)/shard_map/pallas_call | solution.py:351
  19.4 0.6 %slice_bitcast_fusion = (f32[12,32]{1,0:T(8,128)}, f32[12,32]{1,0:T(8,128)}) fusion(f32[2,12,32]{2,1,0:T(8,128)S(1)} %shard_map.149), kind=kLoop, calls=%fused_computation | loop fusion | bytes 6144 | tf_op jit(solution)/shard_map/squeeze | solution.py:390

commit v7 on v6

--- a/solution.py
+++ b/solution.py
@@ -132,17 +132,13 @@
     gain_t = jnp.concatenate([gt_ref[...], gt_ref[...]], axis=1)
     gain_kt = jnp.where(is_text, gain_t, gain_k)
     for c in range((heads + 1) // 2):
-        qn = normed(tall(chunk(q_in, c)), gain_q)
         kn = normed(with_text(chunk(k_in, c), chunk(tk_in, c)), gain_kt)
         vv = with_text(chunk(v_in, c), chunk(tv_in, c))
-        q_turn = pltpu.roll(qn, head_size, 1)
         k_turn = pltpu.roll(kn, head_size, 1)
         v_turn = pltpu.roll(vv, head_size, 1)
         stage[2 * c, 0:tile] = (jnp.where(low, kn, v_turn) + flags).astype(bf16)
-        stage[2 * c, tile:2 * tile] = jnp.where(low, qn, 0.0).astype(bf16)
         if 2 * c + 1 < heads:
             stage[2 * c + 1, 0:tile] = (jnp.where(low, k_turn, vv) + flags).astype(bf16)
-            stage[2 * c + 1, tile:2 * tile] = jnp.where(low, q_turn, 0.0).astype(bf16)
 
     pl.semaphore_wait(barrier, n - 1 + team)
 
@@ -175,6 +171,12 @@
         rolled(0, team, send_far)
 
     each_team(send_team)
+    for c in range((heads + 1) // 2):
+        qn = normed(tall(chunk(q_in, c)), gain_q)
+        stage[2 * c, tile:2 * tile] = jnp.where(low, qn, 0.0).astype(bf16)
+        if 2 * c + 1 < heads:
+            q_turn = pltpu.roll(qn, head_size, 1)
+            stage[2 * c + 1, tile:2 * tile] = jnp.where(low, q_turn, 0.0).astype(bf16)
     for e in range(extras):
         @pl.when(place != e * stride)
         def _():

time: 20.2 us -> 20.2 us (level)
  no operation moved by 1% of the time
where the time goes in v7:
time: 20.2 us; the launch traced here: 20 us
  Pallas kernels  16.8 us (83%)
  between operations  2.58 us (13%)
  local copies, waits for them, and re-layouts  0.61 us (3%)
    pallas_call x1, Pallas kernels, on_device(): pl.pallas_call(functools.partial(exchange_kernel, plan), out_shape=pltpu....  16.8 us
    squeeze x1, local copies, waits for them, and re-layouts, on_device(): return (both[0], both[1])  0.61 us

profile of v7, /device:TPU:0, one launch (start us, length us, event | category | flops | bytes accessed | tf_op | source)
XLA Modules:
  0.0 20.0 jit_solution(16714696519923096456)
XLA Ops:
  2.6 16.8 %shard_map.149 = f32[2,12,32]{2,1,0:T(8,128)S(1)} custom-call(bf16[1,12,1216]{2,1,0:T(8,128)(2,1)} %q_hbm.1, bf16[1,12,1216]{2,1,0:T(8,128)(2,1)} %k_hbm.1, bf16[1,12,1216]{2,1,0:T(8,128)(2,1)} %v_hbm.1, bf16[1,1,1216]{2,1,0:T(2,128)(2,1)} %tk_hbm.1, bf16[1,1,1216]{2,1,0:T(2,128)(2,1)} %tv_hbm.1, f32[1,64]{1,0:T(1,128)} %bitcast.13, f32[1,64]{1,0:T(1,128)} %bitcast.14, ...), custom_call_target="tpu_custom_call" | custom-call | tf_op jit(solution)/shard_map/pallas_call | solution.py:353
  19.4 0.6 %slice_bitcast_fusion = (f32[12,32]{1,0:T(8,128)}, f32[12,32]{1,0:T(8,128)}) fusion(f32[2,12,32]{2,1,0:T(8,128)S(1)} %shard_map.149), kind=kLoop, calls=%fused_computation | loop fusion | bytes 6144 | tf_op jit(solution)/shard_map/squeeze | solution.py:392
